TPU v7x, 256 devices: a whole 4x4x8 slice. The times are simulated.
256 devices in a mesh: dp: 32 (over z, x), cent: 8 (over y, core).
Axes of the slice: x: 4, y: 4, z: 8, core: 2. Of those that a mesh axis runs over, the one named last changes fastest.
Arguments:
- token_embeds: bfloat16 [32768, 128], P(('dp', 'cent')), may hold values from -60 to 60
- centroids: bfloat16 [65536, 128], P('cent'), may hold values from -20 to 20
- targets: int32 [32768], P(('dp', 'cent')), may hold values from 0 to 65535
- token_weights: bfloat16 [32768], P(('dp', 'cent')), may hold values from 1 to 8
Outputs:
- grad_tokens: float32 [32768, 128], P(('dp', 'cent'))
- grad_centroids: float32 [65536, 128], P('cent')
All inputs are finite; a program needn't handle non-finite values.
Results may differ from a plain program's by a relative error of at most 0.00058.
Values may be sent and summed in bfloat16 or wider, within the bound.
No kernel may reach another device: no remote copies, remote signals or barrier semaphores. Data moves between devices by JAX's collectives and lax.ppermute only.
A program may use at most 64 MiB of HBM per device.

v0:
```python
import math

import jax
import jax.numpy as jnp
from jax import lax
from jax.sharding import PartitionSpec as P

BLOCK = 1024


def local(token_embeds, centroids, targets, token_weights):
    embed_width = token_embeds.shape[1]
    factor = 1.0 / math.sqrt(embed_width)
    gathered, labels, weights = (
        lax.all_gather(token_embeds, "cent", axis=0, tiled=True),
        lax.all_gather(targets, "cent", axis=0, tiled=True),
        lax.all_gather(token_weights, "cent", axis=0, tiled=True),
    )
    weights_wide = weights.astype(jnp.float32)
    shard_rows = centroids.shape[0]
    blocks = shard_rows // BLOCK
    offset = lax.axis_index("cent") * shard_rows
    group_rows = gathered.shape[0]

    def scores_of(first_row):
        centroid_block = lax.dynamic_slice_in_dim(centroids, first_row, BLOCK, 0)
        logits = (
            lax.dot_general(
                gathered,
                centroid_block,
                (((1,), (1,)), ((), ())),
                preferred_element_type=jnp.float32,
            )
            * factor
        )
        return (centroid_block, logits)

    def first_pass(carried, block_index):
        row_peak, row_sum = carried
        centroid_block, logits = scores_of(block_index * BLOCK)
        peak_new = jnp.maximum(row_peak, jnp.max(logits, axis=1))
        row_sum = row_sum * jnp.exp(row_peak - peak_new) + jnp.sum(
            jnp.exp(logits - peak_new[:, None]), axis=1
        )
        return ((peak_new, row_sum), None)

    start_state = (
        jnp.full((group_rows,), -jnp.inf, jnp.float32),
        jnp.zeros((group_rows,), jnp.float32),
    )
    (local_peak, local_sum), _ = lax.scan(
        first_pass, start_state, jnp.arange(blocks, dtype=jnp.int32)
    )
    row_peak = lax.pmax(local_peak, "cent")
    row_sum = lax.psum(local_sum * jnp.exp(local_peak - row_peak), "cent")

    def second_pass(token_sum, block_index):
        first_row = block_index * BLOCK
        centroid_block, logits = scores_of(first_row)
        assignment = jnp.exp(logits - row_peak[:, None]) / row_sum[:, None]
        columns = offset + first_row + lax.iota(jnp.int32, BLOCK)
        onehot = (labels[:, None] == columns[None, :]).astype(jnp.float32)
        slopes = (weights_wide[:, None] * (assignment - onehot)).astype(jnp.bfloat16)
        token_sum = token_sum + jnp.dot(slopes, centroid_block, preferred_element_type=jnp.float32)
        grad_block = lax.dot_general(
            slopes, gathered, (((0,), (0,)), ((), ())), preferred_element_type=jnp.float32
        )
        return (token_sum, grad_block)

    token_sum, grad_blocks = lax.scan(
        second_pass,
        jnp.zeros((group_rows, embed_width), jnp.float32),
        jnp.arange(blocks, dtype=jnp.int32),
    )
    token_grad = lax.psum_scatter(token_sum, "cent", scatter_dimension=0, tiled=True) * factor
    centroid_sum = grad_blocks.reshape(shard_rows, embed_width)
    centroid_sum = lax.psum(centroid_sum, "dp")
    return (token_grad, centroid_sum * factor)


def solution(mesh):
    return jax.shard_map(
        local,
        mesh=mesh,
        in_specs=(P(("dp", "cent"), None), P("cent", None), P(("dp", "cent")), P(("dp", "cent"))),
        out_specs=(P(("dp", "cent"), None), P("cent", None)),
        check_vma=False,
    )
```

profile of v0, /device:TPU:1, one launch (start us, length us, event | category | flops | bytes accessed | tf_op | source)
XLA Modules:
  0.0 330.4 jit_solution(11199536177957491452)
XLA Ops:
  8.1 12.2 %all-gather.1 = s32[8,1,128]{2,1,0:T(1,128)S(1)} all-gather(s32[1,1,128]{2,1,0:T(1,128)} %bitcast.43), channel_id=1, replica_groups=mesh['dp'=32,'cent'=8] {'cent'}, dimensions={0}, use_global_device_ids=true | all-gather | bytes 4608 | tf_op jit(solution)/shard_map/all_gather | solution.py:16
  20.3 8.6 %all-gather = bf16[8,1,128]{2,1,0:T(2,128)(2,1)S(1)} all-gather(bf16[1,1,128]{2,1,0:T(2,128)(2,1)} %bitcast.44), channel_id=1, replica_groups=mesh['dp'=32,'cent'=8] {'cent'}, dimensions={0}, use_global_device_ids=true | all-gather | bytes 2304 | tf_op jit(solution)/shard_map/all_gather | solution.py:17
  29.0 13.1 %all_gather.10 = bf16[1024,128]{1,0:T(8,128)(2,1)S(1)} all-gather(bf16[128,128]{1,0:T(8,128)(2,1)} %param.8), channel_id=1, replica_groups=mesh['dp'=32,'cent'=8] {'cent'}, dimensions={0}, use_global_device_ids=true | all-gather | bytes 294912 | tf_op jit(solution)/shard_map/all_gather | solution.py:15
  42.0 28.8 %while.26 = (s32[]{:T(128)}, f32[1024]{0:T(1024)S(1)}, f32[1024]{0:T(1024)S(1)}, s32[8]{0:T(128)S(1)}, bf16[8192,128]{1,0:T(8,128)(2,1)}, /*index=5*/bf16[1024,1...) while((s32[]{:T(128)}, f32[1024]{0:T(1024)S(1)}, f32[1024]{0:T(1024)S(1)}, ...), condition=%wide.region_3.4_spmd.clone, body=%wide.region_0.3_spmd.clone.sunk | while | flops 273683456 | bytes 8966326 | solution.py:51
  70.9 11.9 %pmax.7 = f32[1024]{0:T(1024)S(1)} all-reduce(f32[1024]{0:T(1024)S(1)} %get-tuple-element.93), channel_id=1, replica_groups=mesh['dp'=32,'cent'=8] {'cent'}, use_global_device_ids=true, to_apply=%region_4.5 | all-reduce | flops 1024 | bytes 8192 | tf_op jit(solution)/shard_map/pmax | solution.py:54
  82.8 13.6 %psum.14 = f32[1024]{0:T(1024)S(1)} all-reduce(f32[1024]{0:T(1024)S(1)} %exponential_multiply_fusion), channel_id=1, replica_groups=mesh['dp'=32,'cent'=8] {'cent'}, use_global_device_ids=true, to_apply=%region_5.6 | all-reduce | flops 1024 | bytes 8192 | tf_op jit(solution)/shard_map/psum | solution.py:55
  96.4 55.1 %while.27 = (s32[]{:T(128)}, f32[1024,128]{1,0:T(8,128)S(1)}, f32[8,1024,128]{2,1,0:T(8,128)}, f32[1024]{0:T(1024)S(1)}, s32[8]{0:T(128)S(1)}, /*index=5*/bf16[8...) while((s32[]{:T(128)}, f32[1024,128]{1,0:T(8,128)S(1)}, ...), condition=%wide.region_7.8_spmd.clone, body=%wide.region_6.7_spmd.clone.sunk | while | flops 813958144 | bytes 8937717 | solution.py:70
  97.6 2.4 fusion.34
  100.0 1.8 convolution_add_fusion.2
  104.5 2.4 fusion.34
  106.9 1.8 convolution_add_fusion.2
  111.4 2.4 fusion.34
  113.8 1.8 convolution_add_fusion.2
  118.3 2.4 fusion.34
  120.7 1.8 convolution_add_fusion.2
  125.2 2.4 fusion.34
  127.6 1.8 convolution_add_fusion.2
  132.1 2.4 fusion.34
  134.5 1.8 convolution_add_fusion.2
  139.0 2.4 fusion.34
  145.8 2.4 fusion.34
  153.0 31.6 %reduce-scatter.2.cloned.1.call-done = f32[128,128]{1,0:T(8,128)} async-done(((f32[1024,128]{1,0:T(8,128)}), f32[128,128]{1,0:T(8,128)}) %reduce-scatter.2.cloned.1.call-update) | async-done | bytes 65552 | tf_op jit(solution)/shard_map/reduce_scatter | solution.py:75
  186.0 132.4 %all-reduce.2.cloned.1.call-done = f32[8192,128]{1,0:T(8,128)} async-done(((f32[8192,128]{1,0:T(8,128)}), f32[8192,128]{1,0:T(8,128)}) %all-reduce.2.cloned.1.call-update) | async-done | bytes 4194320 | tf_op jit(solution)/shard_map/psum | solution.py:77
  318.4 4.6 %broadcast_multiply_fusion = f32[8192,128]{1,0:T(8,128)} fusion(f32[8192,128]{1,0:T(8,128)} %all-reduce.2.cloned.1.call-done), kind=kLoop, calls=%fused_computation.19 | loop fusion | flops 1048576 | bytes 8388608 | tf_op jit(solution)/shard_map/mul | solution.py:78
  (89 shorter events, 47.2 us)
Async XLA Ops:
  8.0 176.6 %reduce-scatter.2.cloned.1.call-start = ((), (), s32[]{:S(2)}) async-start(), calls=%async_computation.1 | async-start | bytes 589824 | tf_op jit(solution)/shard_map/reduce_scatter | solution.py:75
  151.6 0.8 copy-start
  152.4 166.0 %all-reduce.2.cloned.1.call-start = ((), (), s32[]{:S(2)}) async-start(), calls=%async_computation.2 | async-start | bytes 8388608 | tf_op jit(solution)/shard_map/psum | solution.py:77
Sparse Core Ops, SparseCore 0:
  152.5 32.0 reduce-scatter.1
Sparse Core Ops, SparseCore 1:
  157.5 160.9 all-reduce.1
where the time goes:
time: 334 us; the launch traced here: 330 us
  waiting for transfers between devices  164 us (49%)
  blocking collectives  59.5 us (18%)
  matrix products  59 us (18%)
  between operations  15.5 us (5%)
  other arithmetic  12.1 us (4%)
  local copies, waits for them, and re-layouts  10.1 us (3%)
  loops' own time  9.62 us (3%)
    psum x1, waiting for transfers between devices, local(): centroid_sum = lax.psum(centroid_sum, 'dp')  132 us
    dot_general x16, matrix products, scores_of(): lax.dot_general(gathered, centroid_block, (((1,), (1,)), ((), ())), prefe...  32.6 us
    reduce_scatter x1, waiting for transfers between devices, local(): lax.psum_scatter(token_sum, 'cent', scatter_dimension=0, tiled=True)  31.6 us
    dot_general x8, matrix products, second_pass(): jnp.dot(slopes, centroid_block, preferred_element_type=jnp.float32)  14.3 us
    psum x1, blocking collectives, local(): row_sum = lax.psum(local_sum * jnp.exp(local_peak - row_peak), 'cent')  13.6 us
    all_gather x1, blocking collectives, local(): lax.all_gather(token_embeds, 'cent', axis=0, tiled=True)  13.1 us
    all_gather x1, blocking collectives, local(): lax.all_gather(targets, 'cent', axis=0, tiled=True)  12.2 us
    dot_general x8, matrix products, second_pass(): lax.dot_general(slopes, gathered, (((0,), (0,)), ((), ())), preferred_ele...  12.1 us
  transfers between devices with their start and end apart: 2, of which 2 were waited for; matrix products, arithmetic and copies ran while one was open for 0% of the time, Pallas kernels for 0%

commit v1 on v0

v1 whole, which is shorter than its diff:
```python
import math

import jax
import jax.numpy as jnp
from jax import lax
from jax.sharding import PartitionSpec as P
from jax.experimental import pallas as pl
from jax.experimental.pallas import tpu as pltpu
A2 = math.log2(math.e) / math.sqrt(128.0)
F32=jnp.float32; BF=jnp.bfloat16
NT=(((1,),(1,)),((),()))

def p1_kernel(cc, g_ref, c_ref, out_ref, e_s, la, lb):
    for j in range(8):
        e_s[j*128:(j+1)*128,:] = g_ref[j,:128,:]
    e=e_s[...]
    n=c_ref.shape[0]//cc
    T=1024
    def dot(i, dst):
        c=c_ref[pl.ds(pl.multiple_of(i*cc,cc),cc),:]
        dst[...]=lax.dot_general(c,e,NT,preferred_element_type=F32)
    def proc(src,m,s):
        l=src[...].reshape(cc//8,8,T)
        mn=jnp.maximum(m,jnp.max(l,axis=0))
        p=jnp.exp2((l-mn[None])*A2)
        s=s*jnp.exp2((m-mn)*A2)+jnp.sum(p,axis=0)
        return mn,s
    dot(0,la)
    def body(k,ms):
        m,s=ms
        dot(2*k+1,lb)
        m,s=proc(la,m,s)
        dot(jnp.minimum(2*k+2,n-1),la)
        m,s=proc(lb,m,s)
        return m,s
    m0=jnp.full((8,T),-3.0e38,F32); s0=jnp.zeros((8,T),F32)
    m,s=lax.fori_loop(0,n//2,body,(m0,s0))
    mt=jnp.max(m,axis=0,keepdims=True)
    st=jnp.sum(s*jnp.exp2((m-mt)*A2),axis=0,keepdims=True)
    for j in range(8):
        out_ref[j:j+1,:]=mt[:,j*128:(j+1)*128]
        out_ref[8+j:9+j,:]=st[:,j*128:(j+1)*128]

def p1(g,cen,cc=512):
    return pl.pallas_call(
        lambda *r: p1_kernel(cc,*r),
        out_shape=jax.ShapeDtypeStruct((16,128),F32),
        scratch_shapes=[pltpu.VMEM((1024,128),BF),pltpu.VMEM((cc,1024),F32),pltpu.VMEM((cc,1024),F32)],
        compiler_params=pltpu.CompilerParams(vmem_limit_bytes=56*2**20),
        cost_estimate=pl.CostEstimate(flops=2*1024*8192*128,bytes_accessed=3*2**20,transcendentals=1024*8192),
        name="pass_one")(g,cen)

def encode(x, half):
    mx=jnp.max(jnp.abs(x),axis=0,keepdims=True)
    k=jnp.ceil(jnp.log2(jnp.maximum(mx,1e-35))*32.0)
    q=jnp.round(x*(jnp.exp2(k*(-1.0/32.0))*32700.0)).astype(jnp.int32)
    code=(q[:half]&0xFFFF)|(q[half:]<<16)
    return code,k.astype(jnp.int32)

def decode(code,k):
    sc=jnp.exp2(k.astype(F32)*(1.0/32.0))*(1.0/32700.0)
    lo=((code<<16)>>16).astype(F32)*sc
    hi=(code>>16).astype(F32)*sc
    return lo,hi

def p2_kernel(cc,tb,base_ref,g_ref,st_ref,c_ref,gc_ref,gt_ref,e_s,ct_s,M,R,W,TG,gcs,gts,la,lb,sa,sb):
    T=4096; C=c_ref.shape[0]
    io=lax.broadcasted_iota(jnp.int32,(8,128),0)
    base=base_ref[1]
    for xx in range(4):
        ms=[st_ref[xx*8+i,0:8,:] for i in range(8)]
        mm=ms[0]
        for v in ms[1:]: mm=jnp.maximum(mm,v)
        ss=sum(st_ref[xx*8+i,8:16,:]*jnp.exp2((ms[i]-mm)*A2) for i in range(8))
        for j in range(8):
            b=xx*8+j; sl=slice(b*128,(b+1)*128)
            e_s[sl,:]=g_ref[xx,j,:128,:]
            info=g_ref[xx,j,128:144,:].astype(F32)
            w=info[0:1,:]
            tg=(info[1:2,:]*256.0+info[2:3,:]).astype(jnp.int32)
            M[:,sl]=jnp.broadcast_to(mm[j:j+1,:],(8,128))
            R[:,sl]=jnp.broadcast_to(w/ss[j:j+1,:],(8,128))
            W[:,sl]=jnp.broadcast_to(w,(8,128))
            TG[:,sl]=jnp.broadcast_to(tg,(8,128))-io-base
    ct_s[...]=c_ref[...].T
    gts[...]=jnp.zeros_like(gts)
    nt=T//tb; n=(C//cc)*nt
    def ix(i):
        return pl.multiple_of((i//nt)*cc,cc), pl.multiple_of((i%nt)*tb,tb)
    def dot(i,dst):
        ci,ti=ix(i)
        dst[...]=lax.dot_general(c_ref[pl.ds(ci,cc),:],e_s[pl.ds(ti,tb),:],NT,preferred_element_type=F32)
    def proc(i,src,dst):
        ci,ti=ix(i); ts=pl.ds(ti,tb)
        l=src[...].reshape(cc//8,8,tb)
        p=jnp.exp2((l-M[:,ts][None])*A2)*R[:,ts][None]
        tgr=TG[:,ts]-ci
        k8=lax.broadcasted_iota(jnp.int32,(cc//8,8,tb),0)*8
        p=p-jnp.where(tgr[None]==k8,W[:,ts][None],0.0)
        dst[...]=p.reshape(cc,tb).astype(BF)
    def mm(i,src):
        ci,ti=ix(i)
        s=src[...]
        d=jnp.dot(s,e_s[pl.ds(ti,tb),:],preferred_element_type=F32)
        @pl.when(i%nt==0)
        def _(): gcs[pl.ds(ci,cc),:]=d
        @pl.when(i%nt!=0)
        def _(): gcs[pl.ds(ci,cc),:]+=d
        gts[:,pl.ds(ti,tb)]+=jnp.dot(ct_s[:,pl.ds(ci,cc)],s,preferred_element_type=F32)
    dot(0,la)
    def body(k,_):
        dot(2*k+1,lb)
        proc(2*k,la,sa)
        mm(2*k,sa)
        dot(jnp.minimum(2*k+2,n-1),la)
        proc(2*k+1,lb,sb)
        mm(2*k+1,sb)
        return 0
    lax.fori_loop(0,n//2,body,0)
    for z in range(8):
        code,k=encode(gcs[z*256:(z+1)*256,:],128)
        gc_ref[z,0:128,:]=code
        gc_ref[z,128:136,:]=jnp.broadcast_to(k,(8,128))
    for b in range(32):
        code,k=encode(gts[:,b*128:(b+1)*128],64)
        gt_ref[b,0:64,:]=code
        gt_ref[b,64:72,:]=jnp.broadcast_to(k,(8,128))

def p2(base,g,st,cen,cc=512,tb=1024):
    T=4096
    return pl.pallas_call(
        lambda *r: p2_kernel(cc,tb,*r),
        out_shape=(jax.ShapeDtypeStruct((8,136,128),jnp.int32),jax.ShapeDtypeStruct((32,72,128),jnp.int32)),
        grid_spec=pltpu.PrefetchScalarGridSpec(num_scalar_prefetch=1,grid=(1,),
            in_specs=[pl.BlockSpec((4,8,144,128),lambda i,b:(0,0,0,0)),
                      pl.BlockSpec((32,16,128),lambda i,b:(0,0,0)),
                      pl.BlockSpec((2048,128),lambda i,b:(b[0],0))],
            out_specs=[pl.BlockSpec((8,136,128),lambda i,b:(0,0,0)),pl.BlockSpec((32,72,128),lambda i,b:(0,0,0))],
            scratch_shapes=[pltpu.VMEM((T,128),BF),pltpu.VMEM((128,2048),BF),
                pltpu.VMEM((8,T),F32),pltpu.VMEM((8,T),F32),pltpu.VMEM((8,T),F32),pltpu.VMEM((8,T),jnp.int32),
                pltpu.VMEM((2048,128),F32),pltpu.VMEM((128,T),F32),
                pltpu.VMEM((cc,tb),F32),pltpu.VMEM((cc,tb),F32),pltpu.VMEM((cc,tb),BF),pltpu.VMEM((cc,tb),BF)]),
        compiler_params=pltpu.CompilerParams(vmem_limit_bytes=56*2**20),
        cost_estimate=pl.CostEstimate(flops=6*4096*2048*128,bytes_accessed=4*2**20,transcendentals=4096*2048),
        name="pass_two")(base,g,st,cen)


def sum_gc_kernel(in_ref, out_ref):
    lo = hi = None
    for z in range(8):
        a, b = decode(in_ref[z, 0:128, :], in_ref[z, 128:129, :])
        lo = a if lo is None else lo + a
        hi = b if hi is None else hi + b
    x = jnp.concatenate([lo, hi], axis=0) * (1.0 / math.sqrt(128.0))
    code, k = encode(x, 128)
    block = jnp.concatenate([code, jnp.broadcast_to(k, (8, 128))], axis=0)
    for z in range(8):
        out_ref[z] = block


def sum_gc(r):
    return pl.pallas_call(
        sum_gc_kernel,
        out_shape=jax.ShapeDtypeStruct((8, 136, 128), jnp.int32),
        cost_estimate=pl.CostEstimate(flops=2**21, bytes_accessed=2**20, transcendentals=0),
        name="sum_centroid_grads",
    )(r)


def narrow_kernel(in_ref, out_ref):
    for z in range(8):
        c = in_ref[z, 0:128, :]
        out_ref[z, 0:128, :] = ((c << 16) >> 16).astype(jnp.int16)
        out_ref[z, 128:256, :] = (c >> 16).astype(jnp.int16)
        k = in_ref[z, 128:136, :]
        out_ref[z, 256:272, :] = jnp.concatenate([k, k], axis=0).astype(jnp.int16)


def narrow(r):
    return pl.pallas_call(
        narrow_kernel,
        out_shape=jax.ShapeDtypeStruct((8, 272, 128), jnp.int16),
        cost_estimate=pl.CostEstimate(flops=2**20, bytes_accessed=2**20, transcendentals=0),
        name="narrow_codes",
    )(r)


def widen_kernel(in_ref, out_ref):
    for z in range(in_ref.shape[0]):
        k = in_ref[z, 256:272, :].astype(F32)[0:1]
        sc = jnp.exp2(k * (1.0 / 32.0)) * (1.0 / 32700.0)
        out_ref[z] = in_ref[z, 0:256, :].astype(F32) * sc


def widen(r, step=4):
    return pl.pallas_call(
        widen_kernel,
        grid=(32 // step,),
        in_specs=[pl.BlockSpec((step, 272, 128), lambda i: (i, 0, 0))],
        out_specs=pl.BlockSpec((step, 256, 128), lambda i: (i, 0, 0)),
        out_shape=jax.ShapeDtypeStruct((32, 256, 128), F32),
        cost_estimate=pl.CostEstimate(flops=2**22, bytes_accessed=6 * 2**20, transcendentals=0),
        name="widen_centroid_grads",
    )(r)


def sum_gt_kernel(in_ref, out_ref):
    lo = hi = None
    for b in range(32):
        a, h = decode(in_ref[b, 0:64, :], in_ref[b, 64:65, :])
        lo = a if lo is None else lo + a
        hi = h if hi is None else hi + h
    x = jnp.concatenate([lo, hi], axis=0) * (1.0 / math.sqrt(128.0))
    out_ref[...] = x.T


def sum_gt(r):
    return pl.pallas_call(
        sum_gt_kernel,
        out_shape=jax.ShapeDtypeStruct((128, 128), F32),
        cost_estimate=pl.CostEstimate(flops=2**20, bytes_accessed=2**20, transcendentals=0),
        name="sum_token_grads",
    )(r)


def spread(x, axes, n):
    return lax.all_to_all(jnp.broadcast_to(x[None], (n,) + x.shape), axes, 0, 0, tiled=True)


def local(token_embeds, centroids, targets, token_weights):
    info = jnp.stack([
        token_weights,
        (targets >> 8).astype(BF),
        (targets & 255).astype(BF),
    ])
    packed = jnp.concatenate([token_embeds, info, jnp.zeros((13, 128), BF)], axis=0)
    group = spread(packed, ("y", "c"), 8)
    plane = spread(group, "x", 4)
    stats = p1(group, centroids)
    all_stats = spread(stats, ("x", "y", "c"), 32)
    x = lax.axis_index("x")
    cent = lax.axis_index("y") * 2 + lax.axis_index("c")
    place = jnp.stack([x, cent * 8192 + x * 2048]).astype(jnp.int32)
    gc_codes, gt_codes = p2(place, plane, all_stats, centroids)
    gc_parts = lax.all_to_all(gc_codes, "z", 0, 0, tiled=True)
    gt_parts = lax.all_to_all(gt_codes, ("x", "y", "c"), 0, 0, tiled=True)
    gc_rows = sum_gc(gc_parts)
    gc_plane = lax.all_to_all(gc_rows, "z", 0, 0, tiled=True)
    gc_all = lax.all_gather(narrow(gc_plane), "x", axis=0, tiled=True)
    grad_centroids = widen(gc_all).reshape(8192, 128)
    grad_tokens = sum_gt(gt_parts)
    return grad_tokens, grad_centroids


def solution(mesh):
    torus = jax.sharding.Mesh(mesh.devices.reshape(8, 4, 4, 2), ("z", "x", "y", "c"))
    return jax.shard_map(
        local,
        mesh=torus,
        in_specs=(P(("z", "x", "y", "c"), None), P(("y", "c"), None), P(("z", "x", "y", "c")), P(("z", "x", "y", "c"))),
        out_specs=(P(("z", "x", "y", "c"), None), P(("y", "c"), None)),
        check_vma=False,
    )
```

time: 334 us -> 193 us (0.58)
  waiting for transfers between devices: 164 us -> 48.5 us
  matrix products: 59 us -> 0 us
  Pallas kernels: 0 us -> 44.7 us
  blocking collectives: 59.5 us -> 77.4 us
  between operations: 15.5 us -> 0.7 us
  starting transfers between devices: 0.08 us -> 13.7 us
  other arithmetic: 12.1 us -> 1.24 us
  loops' own time: 9.62 us -> 0 us
  local copies, waits for them, and re-layouts: 10.1 us -> 5.3 us
    psum x1 -> x0, waiting for transfers between devices: 132 us -> none  [local(): centroid_sum = lax.psum(centroid_sum, 'dp')]
    dot_general x32 -> x0, matrix products: 59 us -> none  [the longest x16 32.6 us: scores_of(): lax.dot_general(gathered, centroid_block, (((1,), (1,)), ((), ())), prefe...]
    all_to_all x0 -> x3, blocking collectives: none -> 52.1 us  [the longest x2 27.7 us: spread(): lax.all_to_all(jnp.broadcast_to(x[None], (n,) + x.shape), axes, 0, 0, til...]
    all_to_all x0 -> x3, waiting for transfers between devices: none -> 48.5 us  [the longest x1 16.3 us: local(): gt_parts = lax.all_to_all(gt_codes, ('x', 'y', 'c'), 0, 0, tiled=True)]
    pallas_call x0 -> x6, Pallas kernels: none -> 44.7 us  [the longest x1 21.5 us: p2(): pl.pallas_call(lambda *r: p2_kernel(cc, tb, *r), out_shape=(jax.ShapeDtyp...]
    reduce_scatter x1 -> x0, waiting for transfers between devices: 31.6 us -> none  [local(): lax.psum_scatter(token_sum, 'cent', scatter_dimension=0, tiled=True)]
    all_to_all x0 -> x3, starting transfers between devices: none -> 13.7 us  [the longest x1 6.62 us: local(): gt_parts = lax.all_to_all(gt_codes, ('x', 'y', 'c'), 0, 0, tiled=True)]
    psum x1 -> x0, blocking collectives: 13.6 us -> none  [local(): row_sum = lax.psum(local_sum * jnp.exp(local_peak - row_peak), 'cent')]
  transfers between devices with their start and end apart: 2 -> 3, of which waited for: 2 -> 3; matrix products, arithmetic and copies ran while one was open for 0% -> 0% of each run, Pallas kernels for 0% -> 2%
where the time goes in v1:
time: 193 us; the launch traced here: 191 us
  blocking collectives  77.4 us (40%)
  waiting for transfers between devices  48.5 us (25%)
  Pallas kernels  44.7 us (23%)
  starting transfers between devices  13.7 us (7%)
  local copies, waits for them, and re-layouts  5.3 us (3%)
    all_to_all x2, blocking collectives, spread(): lax.all_to_all(jnp.broadcast_to(x[None], (n,) + x.shape), axes, 0, 0, til...  27.7 us
    all_gather x1, blocking collectives, local(): gc_all = lax.all_gather(narrow(gc_plane), 'x', axis=0, tiled=True)  25.3 us
    all_to_all x1, blocking collectives, local(): gc_parts = lax.all_to_all(gc_codes, 'z', 0, 0, tiled=True)  24.4 us
    pallas_call x1, Pallas kernels, p2(): pl.pallas_call(lambda *r: p2_kernel(cc, tb, *r), out_shape=(jax.ShapeDtyp...  21.5 us
    all_to_all x1, waiting for transfers between devices, local(): gt_parts = lax.all_to_all(gt_codes, ('x', 'y', 'c'), 0, 0, tiled=True)  16.3 us
    all_to_all x1, waiting for transfers between devices, local(): gc_plane = lax.all_to_all(gc_rows, 'z', 0, 0, tiled=True)  16.3 us
    all_to_all x1, waiting for transfers between devices, spread(): lax.all_to_all(jnp.broadcast_to(x[None], (n,) + x.shape), axes, 0, 0, til...  15.8 us
    pallas_call x1, Pallas kernels, p1(): pl.pallas_call(lambda *r: p1_kernel(cc, *r), out_shape=jax.ShapeDtypeStru...  10.7 us
  transfers between devices with their start and end apart: 3, of which 3 were waited for; matrix products, arithmetic and copies ran while one was open for 0% of the time, Pallas kernels for 2%

profile of v1, /device:TPU:1, one launch (start us, length us, event | category | flops | bytes accessed | tf_op | source)
XLA Modules:
  0.0 191.5 jit_solution(17870779790381774896)
XLA Ops:
  0.6 0.7 convert_bitcast_fusion
  1.3 1.6 concatenate.3
  2.9 13.6 %all_to_all.30.r_0_ = bf16[8,144,128]{2,1,0:T(8,128)(2,1)} all-to-all(bf16[8,144,128]{2,1,0:T(8,128)(2,1)S(1)} %broadcast_in_dim.9), channel_id=1, replica_groups=mesh['z'=8,'x'=4,'y'=4,'c'=2] {'y','c'}, dimensions={0} | all-to-all | bytes 589824 | tf_op jit(solution)/shard_map/all_to_all | solution.py:227
  16.5 10.7 %pass_one.1 = f32[16,128]{1,0:T(8,128)} custom-call(bf16[8,144,128]{2,1,0:T(8,128)(2,1)} %all_to_all.30.r_0_, bf16[8192,128]{1,0:T(8,128)(2,1)} %r_3_.1), custom_call_target="tpu_custom_call" | custom-call | flops 2147483648 | bytes 3145728 | tf_op jit(solution)/shard_map/pass_one/pallas_call | solution.py:45
  27.2 0.7 broadcast_in_dim.11
  28.0 14.1 %all_to_all.31.r_2_ = f32[32,16,128]{2,1,0:T(8,128)} all-to-all(f32[32,16,128]{2,1,0:T(8,128)S(1)} %broadcast_in_dim.11), channel_id=1, replica_groups=mesh['z'=8,'x'=4,'y'=4,'c'=2] {'x','y','c'}, dimensions={0} | all-to-all | bytes 524288 | tf_op jit(solution)/shard_map/all_to_all | solution.py:227
  42.0 0.0 copy-done.3
  42.0 1.2 broadcast_in_dim.10
  43.2 3.5 %all-to-all-start.1 = ((bf16[4,8,144,128]{3,2,1,0:T(8,128)(2,1)}), bf16[4,8,144,128]{3,2,1,0:T(8,128)(2,1)S(1)}, u32[]{:S(2)}, u32[]{:S(2)}) async-start(bf16[4,8,144,128]{3,2,1,0:T(8,128)(2,1)} %broadcast_in_dim.10), calls=%async_computation.1 | async-start | bytes 2359296 | tf_op jit(solution)/shard_map/all_to_all | solution.py:227
  46.8 0.6 pad_add_fusion.r_0_
  47.3 15.8 %all-to-all-done.1.r_1_ = bf16[4,8,144,128]{3,2,1,0:T(8,128)(2,1)S(1)} async-done(((bf16[4,8,144,128]{3,2,1,0:T(8,128)(2,1)}), bf16[4,8,144,128]{3,2,1,0:T(8,128)(2,1)S(1)}, u32[]{:S(2)}, u32[]{:S(2)}) %all-to-all-start.1) | async-done | bytes 1179680 | tf_op jit(solution)/shard_map/all_to_all | solution.py:227
  63.2 1.0 copy-done.2
  64.2 21.5 %pass_two.1 = (s32[8,136,128]{2,1,0:T(8,128)}, s32[32,72,128]{2,1,0:T(8,128)}) custom-call(s32[2]{0:T(128)} %pad_add_fusion.r_0_, bf16[4,8,144,128]{3,2,1,0:T(8,128)(2,1)} %copy-done.2, f32[32,16,128]{2,1,0:T(8,128)} %all_to_all.31.r_2_, bf16[8192,128]{1,0:T(8,128)(2,1)} %r_3_.1), custom_call_target="tpu_custom_call" | custom-call | flops 6442450944 | bytes 4194304 | tf_op jit(solution)/shard_map/pass_two/pallas_call | solution.py:131
  85.7 24.4 %all_to_all.32.in_ref = s32[8,136,128]{2,1,0:T(8,128)} all-to-all(s32[8,136,128]{2,1,0:T(8,128)} %get-tuple-element.5), channel_id=1, replica_groups=mesh['z'=8,'x'=4,'y'=4,'c'=2] {'z'}, dimensions={0} | all-to-all | bytes 1114112 | tf_op jit(solution)/shard_map/all_to_all | solution.py:245
  110.1 6.6 %all-to-all-start.3 = ((s32[32,72,128]{2,1,0:T(8,128)}), s32[32,72,128]{2,1,0:T(8,128)S(1)}, u32[]{:S(2)}, u32[]{:S(2)}) async-start(s32[32,72,128]{2,1,0:T(8,128)} %get-tuple-element.4), calls=%async_computation.3 | async-start | bytes 2359296 | tf_op jit(solution)/shard_map/all_to_all | solution.py:246
  116.7 2.1 %sum_centroid_grads.1 = s32[8,136,128]{2,1,0:T(8,128)} custom-call(s32[8,136,128]{2,1,0:T(8,128)} %all_to_all.32.in_ref), custom_call_target="tpu_custom_call" | custom-call | flops 2097152 | bytes 1048576 | tf_op jit(solution)/shard_map/sum_centroid_grads/pallas_call | solution.py:162
  118.8 16.3 %all-to-all-done.3.in_ref = s32[32,72,128]{2,1,0:T(8,128)S(1)} async-done(((s32[32,72,128]{2,1,0:T(8,128)}), s32[32,72,128]{2,1,0:T(8,128)S(1)}, u32[]{:S(2)}, u32[]{:S(2)}) %all-to-all-start.3) | async-done | bytes 1179680 | tf_op jit(solution)/shard_map/all_to_all | solution.py:246
  135.2 3.5 %all-to-all-start.5 = ((s32[8,136,128]{2,1,0:T(8,128)}), s32[8,136,128]{2,1,0:T(8,128)S(1)}, u32[]{:S(2)}, u32[]{:S(2)}) async-start(s32[8,136,128]{2,1,0:T(8,128)} %sum_centroid_grads.1), calls=%async_computation.5 | async-start | bytes 1114112 | tf_op jit(solution)/shard_map/all_to_all | solution.py:248
  138.7 2.3 %sum_token_grads.1 = f32[128,128]{1,0:T(8,128)} custom-call(s32[32,72,128]{2,1,0:T(8,128)} %copy-done), custom_call_target="tpu_custom_call" | custom-call | flops 1048576 | bytes 1048576 | tf_op jit(solution)/shard_map/sum_token_grads/pallas_call | solution.py:218
  141.0 16.3 %all-to-all-done.5.in_ref = s32[8,136,128]{2,1,0:T(8,128)S(1)} async-done(((s32[8,136,128]{2,1,0:T(8,128)}), s32[8,136,128]{2,1,0:T(8,128)S(1)}, u32[]{:S(2)}, u32[]{:S(2)}) %all-to-all-start.5) | async-done | bytes 557088 | tf_op jit(solution)/shard_map/all_to_all | solution.py:248
  157.4 0.8 copy-done.1
  158.2 2.0 %narrow_codes.1 = s16[8,272,128]{2,1,0:T(8,128)(2,1)} custom-call(s32[8,136,128]{2,1,0:T(8,128)} %copy-done.1), custom_call_target="tpu_custom_call" | custom-call | flops 1048576 | bytes 1048576 | tf_op jit(solution)/shard_map/narrow_codes/pallas_call | solution.py:180
  160.1 25.3 %all-gather.1.in_ref = s16[32,272,128]{2,1,0:T(8,128)(2,1)} all-gather(s16[8,272,128]{2,1,0:T(8,128)(2,1)} %narrow_codes.1), channel_id=1, replica_groups=mesh['z'=8,'x'=4,'y'=4,'c'=2] {'x'}, dimensions={0}, use_global_device_ids=true | all-gather | bytes 2785280 | tf_op jit(solution)/shard_map/all_gather | solution.py:249
  185.4 6.1 %widen_centroid_grads.1 = f32[32,256,128]{2,1,0:T(8,128)} custom-call(s16[32,272,128]{2,1,0:T(8,128)(2,1)} %all-gather.1.in_ref), custom_call_target="tpu_custom_call" | custom-call | flops 4194304 | bytes 6291456 | tf_op jit(solution)/shard_map/widen_centroid_grads/pallas_call | solution.py:196
  (7 shorter events, 0.1 us)
Async XLA Ops:
  16.5 25.5 %copy-start.3 = (bf16[8,144,128]{2,1,0:T(8,128)(2,1)S(1)}, bf16[8,144,128]{2,1,0:T(8,128)(2,1)}, u32[]{:S(2)}) copy-start(bf16[8,144,128]{2,1,0:T(8,128)(2,1)} %all_to_all.30.r_0_) | copy-start | bytes 884740
  43.2 20.0 %all-to-all-start.1 = ((bf16[4,8,144,128]{3,2,1,0:T(8,128)(2,1)}), bf16[4,8,144,128]{3,2,1,0:T(8,128)(2,1)S(1)}, u32[]{:S(2)}, u32[]{:S(2)}) async-start(bf16[4,8,144,128]{3,2,1,0:T(8,128)(2,1)} %broadcast_in_dim.10), calls=%async_computation.1 | async-start | bytes 2359296 | tf_op jit(solution)/shard_map/all_to_all | solution.py:227
  63.2 1.0 copy-start.2
  110.1 25.1 %all-to-all-start.3 = ((s32[32,72,128]{2,1,0:T(8,128)}), s32[32,72,128]{2,1,0:T(8,128)S(1)}, u32[]{:S(2)}, u32[]{:S(2)}) async-start(s32[32,72,128]{2,1,0:T(8,128)} %get-tuple-element.4), calls=%async_computation.3 | async-start | bytes 2359296 | tf_op jit(solution)/shard_map/all_to_all | solution.py:246
  135.2 3.5 %copy-start = (s32[32,72,128]{2,1,0:T(8,128)}, s32[32,72,128]{2,1,0:T(8,128)S(1)}, u32[]{:S(2)}) copy-start(s32[32,72,128]{2,1,0:T(8,128)S(1)} %all-to-all-done.3.in_ref) | copy-start | bytes 3538948
  135.2 22.2 %all-to-all-start.5 = ((s32[8,136,128]{2,1,0:T(8,128)}), s32[8,136,128]{2,1,0:T(8,128)S(1)}, u32[]{:S(2)}, u32[]{:S(2)}) async-start(s32[8,136,128]{2,1,0:T(8,128)} %sum_centroid_grads.1), calls=%async_computation.5 | async-start | bytes 1114112 | tf_op jit(solution)/shard_map/all_to_all | solution.py:248
  157.3 0.8 copy-start.1

commit v2 on v0

v2 whole, which is shorter than its diff:
```python
import math

import jax
import jax.numpy as jnp
from jax import lax
from jax.experimental import pallas as pl
from jax.experimental.pallas import tpu as pltpu
from jax.sharding import PartitionSpec as P

SCALE = 1.0 / math.sqrt(128.0)
RATE = math.log2(math.e) / math.sqrt(128.0)
F32 = jnp.float32
BF16 = jnp.bfloat16
TOP = 32700.0
STEPS = 32.0
VM = pl.BlockSpec(memory_space=pltpu.VMEM)


def dot(a, b, ca, cb):
    return lax.dot_general(a, b, (((ca,), (cb,)), ((), ())), preferred_element_type=F32)


def params(mib):
    return pltpu.CompilerParams(vmem_limit_bytes=mib * 2**20)


def cost(flops, transcendentals=0):
    return pl.CostEstimate(flops=flops, bytes_accessed=2**21, transcendentals=transcendentals)


def encode(x):
    largest = jnp.max(jnp.abs(x), axis=0, keepdims=True)
    k = jnp.ceil(jnp.log2(jnp.maximum(largest, 1e-35)) * STEPS)
    q = jnp.round(x * (jnp.exp2(k * (-1.0 / STEPS)) * TOP))
    return q.astype(jnp.int32).astype(jnp.int16), k.astype(jnp.int32).astype(jnp.int16)


def scale_of(k):
    return jnp.exp2(k.astype(F32) * (1.0 / STEPS)) * (1.0 / TOP)


def pass_one_kernel(rows, e_ref, c_ref, info_ref, out_ref, la, lb):
    T = 1024
    n = c_ref.shape[0] // rows

    def fill(i, dst, m):
        c = c_ref[pl.ds(pl.multiple_of(i * rows, rows), rows), :]
        l = dot(c, e_ref[...], 1, 1)
        dst[...] = l
        return jnp.maximum(m, jnp.max(l.reshape(rows // 8, 8, T), axis=0))

    def add(src, s, m_of_s, m):
        l = src[...].reshape(rows // 8, 8, T)
        return s * jnp.exp2((m_of_s - m) * RATE) + jnp.sum(jnp.exp2((l - m[None]) * RATE), axis=0)

    m_old = jnp.full((8, T), -3.0e38, F32)
    s = jnp.zeros((8, T), F32)
    m = fill(0, la, m_old)

    def body(k, state):
        m_old, m, s = state
        m_b = fill(2 * k + 1, lb, m)
        s = add(la, s, m_old, m)
        m_a = fill(jnp.minimum(2 * k + 2, n - 1), la, m_b)
        s = add(lb, s, m, m_b)
        return m_b, m_a, s

    m_old, m, s = lax.fori_loop(0, n // 2 - 1, body, (m_old, m, s))
    m_b = fill(n - 1, lb, m)
    s = add(la, s, m_old, m)
    s = add(lb, s, m, m_b)
    m = m_b
    peak = jnp.max(m, axis=0, keepdims=True)
    total = jnp.sum(s * jnp.exp2((m - peak) * RATE), axis=0, keepdims=True)
    for i in range(8):
        for j in range(8):
            out_ref[i, j : j + 1, :] = peak[:, j * 128 : (j + 1) * 128]
            out_ref[i, 8 + j : 9 + j, :] = total[:, j * 128 : (j + 1) * 128]
        out_ref[i, 16:24, :] = info_ref[...]


def pass_one(e, c, info, rows=1024):
    return pl.pallas_call(
        lambda *r: pass_one_kernel(rows, *r),
        in_specs=[VM] * 3,
        out_specs=VM,
        out_shape=jax.ShapeDtypeStruct((8, 24, 128), F32),
        scratch_shapes=[pltpu.VMEM((rows, 1024), F32)] * 2,
        compiler_params=params(24),
        cost_estimate=cost(8 * 2**30, 2**23),
        name="pass_one",
    )(e, c, info)


def combine_kernel(x_ref, out_ref):
    ms = [x_ref[i, 0:8, :] for i in range(8)]
    m = ms[0]
    for v in ms[1:]:
        m = jnp.maximum(m, v)
    s = sum(x_ref[i, 8:16, :] * jnp.exp2((ms[i] - m) * RATE) for i in range(8))
    for j in range(8):
        w = x_ref[j, 16:17, :]
        out_ref[j, 0:1, :] = m[j : j + 1]
        out_ref[j, 1:2, :] = w / s[j : j + 1]
        out_ref[j, 2:8, :] = x_ref[j, 16:22, :]


def combine(x):
    return pl.pallas_call(
        combine_kernel,
        in_specs=[VM],
        out_specs=VM,
        out_shape=jax.ShapeDtypeStruct((8, 8, 128), F32),
        cost_estimate=cost(2**16),
        name="combine",
    )(x)


def token_kernel(rows, base_ref, e_ref, st_ref, c_ref, out_ref, M, R, W, G, acc, la, lb, sa, sb):
    T = 1024
    n = c_ref.shape[0] // rows
    sub = lax.broadcasted_iota(jnp.int32, (8, 128), 0)
    for j in range(8):
        sl = slice(j * 128, (j + 1) * 128)
        M[:, sl] = jnp.broadcast_to(st_ref[j, 0:1, :], (8, 128))
        R[:, sl] = jnp.broadcast_to(st_ref[j, 1:2, :], (8, 128))
        W[:, sl] = jnp.broadcast_to(st_ref[j, 2:3, :], (8, 128))
        G[:, sl] = jnp.broadcast_to(st_ref[j, 3:4, :], (8, 128)).astype(jnp.int32) - sub - base_ref[0]
    acc[...] = jnp.zeros_like(acc)

    def at(i):
        return pl.ds(pl.multiple_of(i * rows, rows), rows)

    def fill(i, dst):
        dst[...] = dot(c_ref[at(i), :], e_ref[...], 1, 1)

    def slope(i, src, dst):
        l = src[...].reshape(rows // 8, 8, T)
        p = jnp.exp2((l - M[...][None]) * RATE) * R[...][None]
        k8 = lax.broadcasted_iota(jnp.int32, (rows // 8, 8, T), 0) * 8
        p = p - jnp.where((G[...] - i * rows)[None] == k8, W[...][None], 0.0)
        dst[...] = p.reshape(rows, T).astype(BF16)

    def add(i, src):
        acc[...] += dot(c_ref[at(i), :], src[...], 0, 0)

    fill(0, la)
    fill(1, lb)
    slope(0, la, sa)

    def body(k, _):
        fill(2 * k + 2, la)
        slope(2 * k + 1, lb, sb)
        add(2 * k, sa)
        fill(2 * k + 3, lb)
        slope(2 * k + 2, la, sa)
        add(2 * k + 1, sb)
        return 0

    lax.fori_loop(0, n // 2 - 1, body, 0)
    slope(n - 1, lb, sb)
    add(n - 2, sa)
    add(n - 1, sb)
    out_ref[...] = acc[...].T * SCALE


def token_grads(base, e, st, c, rows=1024):
    return pl.pallas_call(
        lambda *r: token_kernel(rows, *r),
        in_specs=[pl.BlockSpec(memory_space=pltpu.SMEM)] + [VM] * 3,
        out_specs=VM,
        out_shape=jax.ShapeDtypeStruct((1024, 128), F32),
        scratch_shapes=[pltpu.VMEM((8, 1024), F32)] * 3
        + [pltpu.VMEM((8, 1024), jnp.int32), pltpu.VMEM((128, 1024), F32)]
        + [pltpu.VMEM((rows, 1024), F32)] * 2
        + [pltpu.VMEM((rows, 1024), BF16)] * 2,
        compiler_params=params(32),
        cost_estimate=cost(12 * 2**30, 2**23),
        name="token_grads",
    )(base, e, st, c)


def centroid_kernel(T, base_ref, e0, e1, e2, e3, s0, s1, s2, s3, c_ref, out_ref, E, ET, ST, acc, la, lb, sa, sb):
    N = 2048
    n = 4096 // T
    c = c_ref[pl.ds(pl.multiple_of(base_ref[1], N), N), :]
    for x, (e, s) in enumerate(((e0, s0), (e1, s1), (e2, s2), (e3, s3))):
        E[x * 1024 : (x + 1) * 1024, :] = e[...]
        for j in range(8):
            b = x * 8 + j
            ST[b * 128 : (b + 1) * 128, :] = s[j].T
        ET[:, x * 1024 : (x + 1) * 1024] = e[...].T
    acc[...] = jnp.zeros_like(acc)
    base = base_ref[0] + base_ref[1]

    def at(i):
        return pl.ds(pl.multiple_of(i * T, T), T)

    def fill(i, dst):
        dst[...] = dot(E[at(i), :], c, 1, 1)

    def slope(i, src, dst):
        st = ST[at(i), :]
        p = jnp.exp2((src[...] - st[:, 0:1]) * RATE) * st[:, 1:2]
        place = lax.broadcasted_iota(jnp.int32, (T, N), 1)
        hit = (st[:, 3:4].astype(jnp.int32) - base) == place
        dst[...] = (p - jnp.where(hit, st[:, 2:3], 0.0)).astype(BF16)

    def add(i, src):
        acc[...] += dot(ET[:, at(i)], src[...], 1, 0)

    fill(0, la)
    fill(1, lb)
    slope(0, la, sa)

    def body(k, _):
        fill(2 * k + 2, la)
        slope(2 * k + 1, lb, sb)
        add(2 * k, sa)
        fill(2 * k + 3, lb)
        slope(2 * k + 2, la, sa)
        add(2 * k + 1, sb)
        return 0

    lax.fori_loop(0, n // 2 - 1, body, 0)
    slope(n - 1, lb, sb)
    add(n - 2, sa)
    add(n - 1, sb)
    for z in range(8):
        q, k = encode(acc[:, z * 256 : (z + 1) * 256])
        out_ref[z, 0:128, :] = q
        out_ref[z, 128:144, :] = jnp.broadcast_to(k, (16, 256))


def centroid_grads(base, es, sts, c, T=512):
    return pl.pallas_call(
        lambda *r: centroid_kernel(T, *r),
        in_specs=[pl.BlockSpec(memory_space=pltpu.SMEM)] + [VM] * 9,
        out_specs=VM,
        out_shape=jax.ShapeDtypeStruct((8, 144, 256), jnp.int16),
        scratch_shapes=[
            pltpu.VMEM((4096, 128), BF16),
            pltpu.VMEM((128, 4096), BF16),
            pltpu.VMEM((4096, 8), F32),
            pltpu.VMEM((128, 2048), F32),
            pltpu.VMEM((T, 2048), F32),
            pltpu.VMEM((T, 2048), F32),
            pltpu.VMEM((T, 2048), BF16),
            pltpu.VMEM((T, 2048), BF16),
        ],
        compiler_params=params(32),
        cost_estimate=cost(12 * 2**30, 2**23),
        name="centroid_grads",
    )(base, *es, *sts, c)


def sum_kernel(in_ref, out_ref):
    total = None
    for z in range(8):
        part = in_ref[z, 0:128, :].astype(F32) * scale_of(in_ref[z, 128:144, :])[0:1]
        total = part if total is None else total + part
    q, k = encode(total.T * SCALE)
    block = jnp.concatenate([q, jnp.broadcast_to(k, (16, 128))], axis=0)
    for z in range(8):
        out_ref[z] = block


def sum_planes(r):
    return pl.pallas_call(
        sum_kernel,
        in_specs=[VM],
        out_specs=VM,
        out_shape=jax.ShapeDtypeStruct((8, 272, 128), jnp.int16),
        cost_estimate=cost(2**22),
        name="sum_planes",
    )(r)


def widen(r):
    return r[:, 0:256, :].astype(F32) * scale_of(r[:, 256:257, :])


def shift(x, k):
    return lax.ppermute(x, "x", [(i, (i + k) % 4) for i in range(4)])


def ring(x):
    return [x, shift(x, 1), shift(x, 3), shift(x, 2)]


def local(token_embeds, centroids, targets, token_weights):
    info = jnp.stack([token_weights.astype(F32), targets.astype(F32)])
    info = jnp.concatenate([info, jnp.zeros((6, 128), F32)], axis=0)
    spread = jnp.broadcast_to(token_embeds[None], (8, 128, 128))
    group = lax.all_to_all(spread, ("y", "c"), 0, 0, tiled=True).reshape(1024, 128)
    plane = ring(group)
    stats = lax.all_to_all(pass_one(group, centroids, info), ("y", "c"), 0, 0, tiled=True)
    stats = combine(stats)
    plane_stats = ring(stats)
    cent = lax.axis_index("y") * 2 + lax.axis_index("c")
    base = jnp.stack([cent * 8192, lax.axis_index("x") * 2048]).astype(jnp.int32)
    token_part = token_grads(base, group, stats, centroids)
    grad_tokens = lax.psum_scatter(token_part, ("y", "c"), scatter_dimension=0, tiled=True)
    codes = centroid_grads(base, plane, plane_stats, centroids)
    codes = sum_planes(lax.all_to_all(codes, "z", 0, 0, tiled=True))
    codes = lax.all_to_all(codes, "z", 0, 0, tiled=True)
    codes = lax.all_gather(codes, "x", axis=0, tiled=True)
    return grad_tokens, widen(codes).reshape(8192, 128)


def solution(mesh):
    torus = jax.sharding.Mesh(mesh.devices.reshape(8, 4, 4, 2), ("z", "x", "y", "c"))
    tokens = P(("z", "x", "y", "c"))
    return jax.shard_map(
        local,
        mesh=torus,
        in_specs=(P(("z", "x", "y", "c"), None), P(("y", "c"), None), tokens, tokens),
        out_specs=(P(("z", "x", "y", "c"), None), P(("y", "c"), None)),
        check_vma=False,
    )
```

time: 334 us -> 157 us (0.47)
  waiting for transfers between devices: 164 us -> 24.3 us
  matrix products: 59 us -> 0 us
  Pallas kernels: 0 us -> 41.3 us
  starting transfers between devices: 0.08 us -> 17.7 us
  blocking collectives: 59.5 us -> 49.1 us
  loops' own time: 9.62 us -> 0 us
  other arithmetic: 12.1 us -> 4.21 us
  local copies, waits for them, and re-layouts: 10.1 us -> 3.94 us
    psum x1 -> x0, waiting for transfers between devices: 132 us -> none  [local(): centroid_sum = lax.psum(centroid_sum, 'dp')]
    dot_general x32 -> x0, matrix products: 59 us -> none  [the longest x16 32.6 us: scores_of(): lax.dot_general(gathered, centroid_block, (((1,), (1,)), ((), ())), prefe...]
    pallas_call x0 -> x5, Pallas kernels: none -> 41.3 us  [the longest x1 15.3 us: centroid_grads(): pl.pallas_call(lambda *r: centroid_kernel(T, *r), in_specs=[pl.BlockSpec(...]
    all_to_all x0 -> x2, blocking collectives: none -> 32.2 us  [the longest x1 22.2 us: local(): codes = sum_planes(lax.all_to_all(codes, 'z', 0, 0, tiled=True))]
    reduce_scatter x1, waiting for transfers between devices: 31.6 us -> 13.6 us  [local(): lax.psum_scatter(token_part, ('y', 'c'), scatter_dimension=0, tiled=True)]
    all_gather x3 -> x1, blocking collectives: 33.9 us -> 17 us  [local(): codes = lax.all_gather(codes, 'x', axis=0, tiled=True)]
    psum x1 -> x0, blocking collectives: 13.6 us -> none  [local(): row_sum = lax.psum(local_sum * jnp.exp(local_peak - row_peak), 'cent')]
    pmax x1 -> x0, blocking collectives: 11.9 us -> none  [local(): row_peak = lax.pmax(local_peak, 'cent')]
  transfers between devices with their start and end apart: 2 -> 9, of which waited for: 2 -> 4; matrix products, arithmetic and copies ran while one was open for 0% -> 3% of each run, Pallas kernels for 0% -> 15%
where the time goes in v2:
time: 157 us; the launch traced here: 155 us
  blocking collectives  49.1 us (31%)
  Pallas kernels  41.3 us (26%)
  waiting for transfers between devices  24.3 us (15%)
  starting transfers between devices  17.7 us (11%)
  between operations  14.1 us (9%)
  other arithmetic  4.21 us (3%)
  local copies, waits for them, and re-layouts  3.94 us (3%)
    all_to_all x1, blocking collectives, local(): codes = sum_planes(lax.all_to_all(codes, 'z', 0, 0, tiled=True))  22.2 us
    all_gather x1, blocking collectives, local(): codes = lax.all_gather(codes, 'x', axis=0, tiled=True)  17 us
    pallas_call x1, Pallas kernels, centroid_grads(): pl.pallas_call(lambda *r: centroid_kernel(T, *r), in_specs=[pl.BlockSpec(...  15.3 us
    pallas_call x1, Pallas kernels, token_grads(): pl.pallas_call(lambda *r: token_kernel(rows, *r), in_specs=[pl.BlockSpec(...  14.1 us
    reduce_scatter x1, waiting for transfers between devices, local(): lax.psum_scatter(token_part, ('y', 'c'), scatter_dimension=0, tiled=True)  13.6 us
    all_to_all x1, blocking collectives, local(): lax.all_to_all(pass_one(group, centroids, info), ('y', 'c'), 0, 0, tiled=...  9.92 us
    pallas_call x1, Pallas kernels, pass_one(): pl.pallas_call(lambda *r: pass_one_kernel(rows, *r), in_specs=[VM] * 3, o...  8.17 us
    ppermute x6, starting transfers between devices, shift(): return lax.ppermute(x, 'x', [(i, (i + k) % 4) for i in range(4)])  6.6 us
  transfers between devices with their start and end apart: 9, of which 4 were waited for; matrix products, arithmetic and copies ran while one was open for 3% of the time, Pallas kernels for 15%

profile of v2, /device:TPU:1, one launch (start us, length us, event | category | flops | bytes accessed | tf_op | source)
XLA Modules:
  0.0 154.6 jit_solution(15325718243275822449)
XLA Ops:
  7.2 1.5 broadcast_in_dim.4
  8.7 6.6 %all-to-all-start = ((bf16[8,128,128]{2,1,0:T(8,128)(2,1)}), bf16[8,128,128]{2,1,0:T(8,128)(2,1)S(1)}, u32[]{:S(2)}, u32[]{:S(2)}) async-start(bf16[8,128,128]{2,1,0:T(8,128)(2,1)} %broadcast_in_dim.4), calls=%async_computation | async-start | bytes 524288 | tf_op jit(solution)/shard_map/all_to_all | solution.py:295
  15.2 0.7 convert_bitcast_fusion
  15.9 0.7 bitcast_convert_fusion
  16.7 5.1 %all-to-all-done = bf16[8,128,128]{2,1,0:T(8,128)(2,1)S(1)} async-done(((bf16[8,128,128]{2,1,0:T(8,128)(2,1)}), bf16[8,128,128]{2,1,0:T(8,128)(2,1)S(1)}, u32[]{:S(2)}, u32[]{:S(2)}) %all-to-all-start) | async-done | bytes 262176 | tf_op jit(solution)/shard_map/all_to_all | solution.py:295
  21.7 2.1 %collective-permute-start.2 = (bf16[1024,128]{1,0:T(8,128)(2,1)S(1)}, bf16[1024,128]{1,0:T(8,128)(2,1)S(1)}, u32[]{:S(2)}, u32[]{:S(2)}) collective-permute-start(bf16[1024,128]{1,0:T(8,128)(2,1)S(1)} %bitcast.11), channel_id=1, source_target_pairs={{0,16},{8,24},{16,0},{24,8},{1,17},{9,25},{17,1},{25,9},{2,18},{10... | collective-permute-start | bytes 786440 | tf_op jit(solution)/shard_map/ppermute | solution.py:284
  23.9 0.9 collective-permute-start.1
  25.3 1.6 %copy-done.2 = bf16[8192,128]{1,0:T(8,128)(2,1)S(1)} copy-done((bf16[8192,128]{1,0:T(8,128)(2,1)S(1)}, bf16[8192,128]{1,0:T(8,128)(2,1)}, u32[]{:S(2)}) %copy-start.2) | copy-done | bytes 2097176
  26.9 8.2 %pass_one.1 = f32[8,24,128]{2,1,0:T(8,128)S(1)} custom-call(bf16[1024,128]{1,0:T(8,128)(2,1)S(1)} %bitcast.14, bf16[8192,128]{1,0:T(8,128)(2,1)S(1)} %copy-done.2, f32[8,128]{1,0:T(8,128)S(1)} %maximum_maximum_fusion.r_2_), custom_call_target="tpu_custom_call" | custom-call | flops 8589934592 | bytes 2097152 | tf_op jit(solution)/shard_map/pass_one/pallas_call | solution.py:83
  35.1 9.9 %all_to_all.20.x_ref = f32[8,24,128]{2,1,0:T(8,128)} all-to-all(f32[8,24,128]{2,1,0:T(8,128)S(1)} %pass_one.1), channel_id=1, replica_groups=mesh['z'=8,'x'=4,'y'=4,'c'=2] {'y','c'}, dimensions={0} | all-to-all | bytes 196608 | tf_op jit(solution)/shard_map/all_to_all | solution.py:297
  45.0 1.5 combine.1.r_2_.r_5_
  46.6 0.8 collective-permute-start.5
  47.4 1.9 %collective-permute-start.4 = (f32[8,8,128]{2,1,0:T(8,128)}, f32[8,8,128]{2,1,0:T(8,128)S(1)}, u32[]{:S(2)}, u32[]{:S(2)}) collective-permute-start(f32[8,8,128]{2,1,0:T(8,128)} %combine.1.r_2_.r_5_), channel_id=1, source_target_pairs={{0,24},{8,0},{16,8},{24,16},{1,25},{9,1},{17,9},{25,17},{2,26},{10... | collective-permute-start | bytes 98312 | tf_op jit(solution)/shard_map/ppermute | solution.py:284
  49.3 1.8 %collective-permute-done.5.r_8_ = f32[8,8,128]{2,1,0:T(8,128)S(1)} collective-permute-done((f32[8,8,128]{2,1,0:T(8,128)}, f32[8,8,128]{2,1,0:T(8,128)S(1)}, u32[]{:S(2)}, u32[]{:S(2)}) %collective-permute-start.5) | collective-permute-done | bytes 32800 | tf_op jit(solution)/shard_map/ppermute | solution.py:284
  51.4 3.8 %collective-permute-done.3.r_6_ = f32[8,8,128]{2,1,0:T(8,128)S(1)} collective-permute-done((f32[8,8,128]{2,1,0:T(8,128)}, f32[8,8,128]{2,1,0:T(8,128)S(1)}, u32[]{:S(2)}, u32[]{:S(2)}) %collective-permute-start.3) | collective-permute-done | bytes 32800 | tf_op jit(solution)/shard_map/ppermute | solution.py:284
  55.3 0.7 copy-done
  56.0 15.3 %centroid_grads.1 = s16[8,144,256]{2,1,0:T(8,128)(2,1)S(1)} custom-call(s32[2]{0:T(128)S(1)} %pad_add_fusion.r_0_, bf16[1024,128]{1,0:T(8,128)(2,1)S(1)} %bitcast.15, bf16[1024,128]{1,0:T(8,128)(2,1)S(1)} %collective-permute-done.r_2_, bf16[1024,128]{1,0:T(8,128)(2,1)S(1)} %collective-permute-done.1.r_3_, bf16[1024,128]{1,0:T(8,128)(2,1)S(1)} %collective-permute-done.2.r_4_, ...), custom_call_target="tpu_custom_call" | custom-call | flops 12884901888 | bytes 2097152 | tf_op jit(solution)/shard_map/centroid_grads/pallas_call | solution.py:236
  71.3 22.2 %all_to_all.21.in_ref = s16[8,144,256]{2,1,0:T(8,128)(2,1)} all-to-all(s16[8,144,256]{2,1,0:T(8,128)(2,1)S(1)} %centroid_grads.1), channel_id=1, replica_groups=mesh['z'=8,'x'=4,'y'=4,'c'=2] {'z'}, dimensions={0} | all-to-all | bytes 1179648 | tf_op jit(solution)/shard_map/all_to_all | solution.py:305
  93.6 2.2 %sum_planes.1 = s16[8,272,128]{2,1,0:T(8,128)(2,1)} custom-call(s16[8,144,256]{2,1,0:T(8,128)(2,1)} %all_to_all.21.in_ref), custom_call_target="tpu_custom_call" | custom-call | flops 4194304 | bytes 2097152 | tf_op jit(solution)/shard_map/sum_planes/pallas_call | solution.py:269
  95.8 4.3 %all-to-all-start.3 = ((s16[8,272,128]{2,1,0:T(8,128)(2,1)}), s16[8,272,128]{2,1,0:T(8,128)(2,1)S(1)}, u32[]{:S(2)}, u32[]{:S(2)}) async-start(s16[8,272,128]{2,1,0:T(8,128)(2,1)} %sum_planes.1), calls=%async_computation.4 | async-start | bytes 1114112 | tf_op jit(solution)/shard_map/all_to_all | solution.py:306
  100.3 14.1 %token_grads.1 = f32[1024,128]{1,0:T(8,128)} custom-call(s32[2]{0:T(128)S(1)} %pad_add_fusion.r_0_, bf16[1024,128]{1,0:T(8,128)(2,1)S(1)} %bitcast.16, f32[8,8,128]{2,1,0:T(8,128)S(1)} %copy-done.1, bf16[8192,128]{1,0:T(8,128)(2,1)S(1)} %copy-done.3), custom_call_target="tpu_custom_call" | custom-call | flops 12884901888 | bytes 2097152 | tf_op jit(solution)/shard_map/token_grads/pallas_call | solution.py:168
  114.4 17.0 %all-gather.1 = s16[32,272,128]{2,1,0:T(8,128)(2,1)S(1)} all-gather(s16[8,272,128]{2,1,0:T(8,128)(2,1)S(1)} %all-to-all-done.3), channel_id=1, replica_groups=mesh['z'=8,'x'=4,'y'=4,'c'=2] {'x'}, dimensions={0}, use_global_device_ids=true | all-gather | bytes 2785280 | tf_op jit(solution)/shard_map/all_gather | solution.py:307
  131.4 2.7 %convert_multiply_fusion = f32[32,256,128]{2,1,0:T(8,128)} fusion(s16[32,272,128]{2,1,0:T(8,128)(2,1)S(1)} %all-gather.1, f32[32,128]{1,0:T(8,128)S(1)} %multiply_bitcast_fusion), kind=kLoop, calls=%fused_computation | loop fusion | flops 2097152 | bytes 6307840 | tf_op jit(solution)/shard_map/mul | solution.py:280
  134.2 13.6 %reduce-scatter.2.cloned.1.call-done = f32[128,128]{1,0:T(8,128)} async-done(((f32[1024,128]{1,0:T(8,128)}), f32[128,128]{1,0:T(8,128)}) %reduce-scatter.2.cloned.1.call-update) | async-done | bytes 65552 | tf_op jit(solution)/shard_map/reduce_scatter | solution.py:303
  (21 shorter events, 1.5 us)
Async XLA Ops:
  8.7 13.1 %all-to-all-start = ((bf16[8,128,128]{2,1,0:T(8,128)(2,1)}), bf16[8,128,128]{2,1,0:T(8,128)(2,1)S(1)}, u32[]{:S(2)}, u32[]{:S(2)}) async-start(bf16[8,128,128]{2,1,0:T(8,128)(2,1)} %broadcast_in_dim.4), calls=%async_computation | async-start | bytes 524288 | tf_op jit(solution)/shard_map/all_to_all | solution.py:295
  21.7 33.5 %collective-permute-start.2 = (bf16[1024,128]{1,0:T(8,128)(2,1)S(1)}, bf16[1024,128]{1,0:T(8,128)(2,1)S(1)}, u32[]{:S(2)}, u32[]{:S(2)}) collective-permute-start(bf16[1024,128]{1,0:T(8,128)(2,1)S(1)} %bitcast.11), channel_id=1, source_target_pairs={{0,16},{8,24},{16,0},{24,8},{1,17},{9,25},{17,1},{25,9},{2,18},{10... | collective-permute-start | bytes 786440 | tf_op jit(solution)/shard_map/ppermute | solution.py:284
  23.9 31.4 %collective-permute-start.1 = (bf16[1024,128]{1,0:T(8,128)(2,1)S(1)}, bf16[1024,128]{1,0:T(8,128)(2,1)S(1)}, u32[]{:S(2)}, u32[]{:S(2)}) collective-permute-start(bf16[1024,128]{1,0:T(8,128)(2,1)S(1)} %bitcast.12), channel_id=1, source_target_pairs={{0,24},{8,0},{16,8},{24,16},{1,25},{9,1},{17,9},{25,17},{2,26},{10... | collective-permute-start | bytes 786440 | tf_op jit(solution)/shard_map/ppermute | solution.py:284
  24.7 30.5 %collective-permute-start = (bf16[1024,128]{1,0:T(8,128)(2,1)S(1)}, bf16[1024,128]{1,0:T(8,128)(2,1)S(1)}, u32[]{:S(2)}, u32[]{:S(2)}) collective-permute-start(bf16[1024,128]{1,0:T(8,128)(2,1)S(1)} %bitcast.13), channel_id=1, source_target_pairs={{0,8},{8,16},{16,24},{24,0},{1,9},{9,17},{17,25},{25,1},{2,10},{10... | collective-permute-start | bytes 786440 | tf_op jit(solution)/shard_map/ppermute | solution.py:284
  25.3 1.6 %copy-start.2 = (bf16[8192,128]{1,0:T(8,128)(2,1)S(1)}, bf16[8192,128]{1,0:T(8,128)(2,1)}, u32[]{:S(2)}) copy-start(bf16[8192,128]{1,0:T(8,128)(2,1)} %r_9_.1) | copy-start | bytes 6291460
  26.9 28.3 %copy-start.3 = (bf16[8192,128]{1,0:T(8,128)(2,1)S(1)}, bf16[8192,128]{1,0:T(8,128)(2,1)}, u32[]{:S(2)}) copy-start(bf16[8192,128]{1,0:T(8,128)(2,1)} %r_9_.1) | copy-start | bytes 6291460
  46.6 4.5 %collective-permute-start.5 = (f32[8,8,128]{2,1,0:T(8,128)}, f32[8,8,128]{2,1,0:T(8,128)S(1)}, u32[]{:S(2)}, u32[]{:S(2)}) collective-permute-start(f32[8,8,128]{2,1,0:T(8,128)} %combine.1.r_2_.r_5_), channel_id=1, source_target_pairs={{0,16},{8,24},{16,0},{24,8},{1,17},{9,25},{17,1},{25,9},{2,18},{10... | collective-permute-start | bytes 98312 | tf_op jit(solution)/shard_map/ppermute | solution.py:284
  47.4 4.0 %collective-permute-start.4 = (f32[8,8,128]{2,1,0:T(8,128)}, f32[8,8,128]{2,1,0:T(8,128)S(1)}, u32[]{:S(2)}, u32[]{:S(2)}) collective-permute-start(f32[8,8,128]{2,1,0:T(8,128)} %combine.1.r_2_.r_5_), channel_id=1, source_target_pairs={{0,24},{8,0},{16,8},{24,16},{1,25},{9,1},{17,9},{25,17},{2,26},{10... | collective-permute-start | bytes 98312 | tf_op jit(solution)/shard_map/ppermute | solution.py:284
  51.1 4.2 %collective-permute-start.3 = (f32[8,8,128]{2,1,0:T(8,128)}, f32[8,8,128]{2,1,0:T(8,128)S(1)}, u32[]{:S(2)}, u32[]{:S(2)}) collective-permute-start(f32[8,8,128]{2,1,0:T(8,128)} %combine.1.r_2_.r_5_), channel_id=1, source_target_pairs={{0,8},{8,16},{16,24},{24,0},{1,9},{9,17},{17,25},{25,1},{2,10},{10... | collective-permute-start | bytes 98312 | tf_op jit(solution)/shard_map/ppermute | solution.py:284
  55.3 0.8 copy-start
  56.0 44.3 %copy-start.1 = (f32[8,8,128]{2,1,0:T(8,128)S(1)}, f32[8,8,128]{2,1,0:T(8,128)}, u32[]{:S(2)}) copy-start(f32[8,8,128]{2,1,0:T(8,128)} %combine.1.r_2_.r_5_) | copy-start | bytes 98308
  95.8 18.7 %all-to-all-start.3 = ((s16[8,272,128]{2,1,0:T(8,128)(2,1)}), s16[8,272,128]{2,1,0:T(8,128)(2,1)S(1)}, u32[]{:S(2)}, u32[]{:S(2)}) async-start(s16[8,272,128]{2,1,0:T(8,128)(2,1)} %sum_planes.1), calls=%async_computation.4 | async-start | bytes 1114112 | tf_op jit(solution)/shard_map/all_to_all | solution.py:306
  100.0 47.8 %reduce-scatter.2.cloned.1.call-start = ((), (), s32[]{:S(2)}) async-start(), calls=%async_computation.5 | async-start | bytes 589824 | tf_op jit(solution)/shard_map/reduce_scatter | solution.py:303
Sparse Core Ops, SparseCore 0:
  114.5 33.1 reduce-scatter.1

commit v3 on v2

--- a/solution.py
+++ b/solution.py
@@ -72,10 +72,12 @@
     m = m_b
     peak = jnp.max(m, axis=0, keepdims=True)
     total = jnp.sum(s * jnp.exp2((m - peak) * RATE), axis=0, keepdims=True)
-    for i in range(8):
-        for j in range(8):
-            out_ref[i, j : j + 1, :] = peak[:, j * 128 : (j + 1) * 128]
-            out_ref[i, 8 + j : 9 + j, :] = total[:, j * 128 : (j + 1) * 128]
+    cut = [slice(j * 128, (j + 1) * 128) for j in range(8)]
+    peaks = jnp.concatenate([peak[:, c] for c in cut], axis=0)
+    totals = jnp.concatenate([total[:, c] for c in cut], axis=0)
+    for i in range(32):
+        out_ref[i, 0:8, :] = peaks
+        out_ref[i, 8:16, :] = totals
         out_ref[i, 16:24, :] = info_ref[...]
 
 
@@ -84,7 +86,7 @@
         lambda *r: pass_one_kernel(rows, *r),
         in_specs=[VM] * 3,
         out_specs=VM,
-        out_shape=jax.ShapeDtypeStruct((8, 24, 128), F32),
+        out_shape=jax.ShapeDtypeStruct((32, 24, 128), F32),
         scratch_shapes=[pltpu.VMEM((rows, 1024), F32)] * 2,
         compiler_params=params(24),
         cost_estimate=cost(8 * 2**30, 2**23),
@@ -92,40 +94,28 @@
     )(e, c, info)
 
 
-def combine_kernel(x_ref, out_ref):
-    ms = [x_ref[i, 0:8, :] for i in range(8)]
-    m = ms[0]
-    for v in ms[1:]:
-        m = jnp.maximum(m, v)
-    s = sum(x_ref[i, 8:16, :] * jnp.exp2((ms[i] - m) * RATE) for i in range(8))
-    for j in range(8):
-        w = x_ref[j, 16:17, :]
-        out_ref[j, 0:1, :] = m[j : j + 1]
-        out_ref[j, 1:2, :] = w / s[j : j + 1]
-        out_ref[j, 2:8, :] = x_ref[j, 16:22, :]
-
-
-def combine(x):
-    return pl.pallas_call(
-        combine_kernel,
-        in_specs=[VM],
-        out_specs=VM,
-        out_shape=jax.ShapeDtypeStruct((8, 8, 128), F32),
-        cost_estimate=cost(2**16),
-        name="combine",
-    )(x)
+def combine(x_ref, x):
+    parts = [x_ref[x * 8 + i] for i in range(8)]
+    m = parts[0][0:8]
+    for v in parts[1:]:
+        m = jnp.maximum(m, v[0:8])
+    s = sum(v[8:16] * jnp.exp2((v[0:8] - m) * RATE) for v in parts)
+    w = jnp.concatenate([v[16:17] for v in parts], axis=0)
+    g = jnp.concatenate([v[17:18] for v in parts], axis=0)
+    return m, w / s, w, g
 
 
 def token_kernel(rows, base_ref, e_ref, st_ref, c_ref, out_ref, M, R, W, G, acc, la, lb, sa, sb):
     T = 1024
     n = c_ref.shape[0] // rows
     sub = lax.broadcasted_iota(jnp.int32, (8, 128), 0)
+    m, r, w, g = combine(st_ref, base_ref[2])
     for j in range(8):
         sl = slice(j * 128, (j + 1) * 128)
-        M[:, sl] = jnp.broadcast_to(st_ref[j, 0:1, :], (8, 128))
-        R[:, sl] = jnp.broadcast_to(st_ref[j, 1:2, :], (8, 128))
-        W[:, sl] = jnp.broadcast_to(st_ref[j, 2:3, :], (8, 128))
-        G[:, sl] = jnp.broadcast_to(st_ref[j, 3:4, :], (8, 128)).astype(jnp.int32) - sub - base_ref[0]
+        M[:, sl] = jnp.broadcast_to(m[j : j + 1], (8, 128))
+        R[:, sl] = jnp.broadcast_to(r[j : j + 1], (8, 128))
+        W[:, sl] = jnp.broadcast_to(w[j : j + 1], (8, 128))
+        G[:, sl] = jnp.broadcast_to(g[j : j + 1], (8, 128)).astype(jnp.int32) - sub - base_ref[0]
     acc[...] = jnp.zeros_like(acc)
 
     def at(i):
@@ -161,34 +151,39 @@
     slope(n - 1, lb, sb)
     add(n - 2, sa)
     add(n - 1, sb)
-    out_ref[...] = acc[...].T * SCALE
-
-
-def token_grads(base, e, st, c, rows=1024):
+    for j in range(8):
+        q, k = encode(acc[:, j * 128 : (j + 1) * 128])
+        out_ref[j, 0:128, :] = q
+        out_ref[j, 128:144, :] = jnp.broadcast_to(k, (16, 128))
+
+
+def token_grads(base, e, st, c, rows=2048):
     return pl.pallas_call(
         lambda *r: token_kernel(rows, *r),
         in_specs=[pl.BlockSpec(memory_space=pltpu.SMEM)] + [VM] * 3,
         out_specs=VM,
-        out_shape=jax.ShapeDtypeStruct((1024, 128), F32),
+        out_shape=jax.ShapeDtypeStruct((8, 144, 128), jnp.int16),
         scratch_shapes=[pltpu.VMEM((8, 1024), F32)] * 3
         + [pltpu.VMEM((8, 1024), jnp.int32), pltpu.VMEM((128, 1024), F32)]
         + [pltpu.VMEM((rows, 1024), F32)] * 2
         + [pltpu.VMEM((rows, 1024), BF16)] * 2,
-        compiler_params=params(32),
+        compiler_params=params(40),
         cost_estimate=cost(12 * 2**30, 2**23),
         name="token_grads",
     )(base, e, st, c)
 
 
-def centroid_kernel(T, base_ref, e0, e1, e2, e3, s0, s1, s2, s3, c_ref, out_ref, E, ET, ST, acc, la, lb, sa, sb):
+def centroid_kernel(T, base_ref, e0, e1, e2, e3, st_ref, c_ref, out_ref, E, ET, ST, acc, la, lb, sa, sb):
     N = 2048
     n = 4096 // T
     c = c_ref[pl.ds(pl.multiple_of(base_ref[1], N), N), :]
-    for x, (e, s) in enumerate(((e0, s0), (e1, s1), (e2, s2), (e3, s3))):
+    for x, (e, step) in enumerate(((e0, 0), (e1, 3), (e2, 1), (e3, 2))):
         E[x * 1024 : (x + 1) * 1024, :] = e[...]
+        stats = combine(st_ref, lax.rem(base_ref[2] + step, 4))
         for j in range(8):
             b = x * 8 + j
-            ST[b * 128 : (b + 1) * 128, :] = s[j].T
+            tile = jnp.concatenate([v[j : j + 1] for v in stats] + [jnp.zeros((4, 128), F32)], axis=0)
+            ST[b * 128 : (b + 1) * 128, :] = tile.T
         ET[:, x * 1024 : (x + 1) * 1024] = e[...].T
     acc[...] = jnp.zeros_like(acc)
     base = base_ref[0] + base_ref[1]
@@ -232,10 +227,10 @@
         out_ref[z, 128:144, :] = jnp.broadcast_to(k, (16, 256))
 
 
-def centroid_grads(base, es, sts, c, T=512):
+def centroid_grads(base, es, st, c, T=1024):
     return pl.pallas_call(
         lambda *r: centroid_kernel(T, *r),
-        in_specs=[pl.BlockSpec(memory_space=pltpu.SMEM)] + [VM] * 9,
+        in_specs=[pl.BlockSpec(memory_space=pltpu.SMEM)] + [VM] * 6,
         out_specs=VM,
         out_shape=jax.ShapeDtypeStruct((8, 144, 256), jnp.int16),
         scratch_shapes=[
@@ -248,18 +243,37 @@
             pltpu.VMEM((T, 2048), BF16),
             pltpu.VMEM((T, 2048), BF16),
         ],
-        compiler_params=params(32),
+        compiler_params=params(48),
         cost_estimate=cost(12 * 2**30, 2**23),
         name="centroid_grads",
-    )(base, *es, *sts, c)
+    )(base, *es, st, c)
+
+
+def total_of(parts):
+    total = None
+    for ref in parts:
+        part = ref[0:128, :].astype(F32) * scale_of(ref[128:144, :])[0:1]
+        total = part if total is None else total + part
+    return total.T * SCALE
+
+
+def sum_tokens_kernel(*refs):
+    refs[8][...] = total_of(refs[:8])
+
+
+def sum_tokens(r):
+    return pl.pallas_call(
+        sum_tokens_kernel,
+        in_specs=[VM] * 8,
+        out_specs=VM,
+        out_shape=jax.ShapeDtypeStruct((128, 128), F32),
+        cost_estimate=cost(2**18),
+        name="sum_tokens",
+    )(*r)
 
 
 def sum_kernel(in_ref, out_ref):
-    total = None
-    for z in range(8):
-        part = in_ref[z, 0:128, :].astype(F32) * scale_of(in_ref[z, 128:144, :])[0:1]
-        total = part if total is None else total + part
-    q, k = encode(total.T * SCALE)
+    q, k = encode(total_of([in_ref.at[z] for z in range(8)]))
     block = jnp.concatenate([q, jnp.broadcast_to(k, (16, 128))], axis=0)
     for z in range(8):
         out_ref[z] = block
@@ -286,6 +300,14 @@
 
 def ring(x):
     return [x, shift(x, 1), shift(x, 3), shift(x, 2)]
+
+
+def exchange(x, me):
+    out = [lax.dynamic_index_in_dim(x, me, 0, keepdims=False)]
+    for k in range(1, 8):
+        block = lax.dynamic_index_in_dim(x, me ^ k, 0, keepdims=False)
+        out.append(lax.ppermute(block, ("y", "c"), [(i, i ^ k) for i in range(8)]))
+    return out
 
 
 def local(token_embeds, centroids, targets, token_weights):
@@ -294,18 +316,21 @@
     spread = jnp.broadcast_to(token_embeds[None], (8, 128, 128))
     group = lax.all_to_all(spread, ("y", "c"), 0, 0, tiled=True).reshape(1024, 128)
     plane = ring(group)
-    stats = lax.all_to_all(pass_one(group, centroids, info), ("y", "c"), 0, 0, tiled=True)
-    stats = combine(stats)
-    plane_stats = ring(stats)
+    stats = pass_one(group, centroids, info)
+    stats, *plane = lax.optimization_barrier((stats, *plane))
+    stats = lax.all_to_all(stats, ("x", "y", "c"), 0, 0, tiled=True)
     cent = lax.axis_index("y") * 2 + lax.axis_index("c")
-    base = jnp.stack([cent * 8192, lax.axis_index("x") * 2048]).astype(jnp.int32)
-    token_part = token_grads(base, group, stats, centroids)
-    grad_tokens = lax.psum_scatter(token_part, ("y", "c"), scatter_dimension=0, tiled=True)
-    codes = centroid_grads(base, plane, plane_stats, centroids)
-    codes = sum_planes(lax.all_to_all(codes, "z", 0, 0, tiled=True))
+    x = lax.axis_index("x")
+    base = jnp.stack([cent * 8192, x * 2048, x]).astype(jnp.int32)
+    codes = centroid_grads(base, plane, stats, centroids)
+    codes = lax.all_to_all(codes, "z", 0, 0, tiled=True)
+    token_codes = token_grads(base, group, stats, centroids)
+    codes = sum_planes(codes)
+    codes, token_codes = lax.optimization_barrier((codes, token_codes))
+    parts = exchange(token_codes, cent)
     codes = lax.all_to_all(codes, "z", 0, 0, tiled=True)
     codes = lax.all_gather(codes, "x", axis=0, tiled=True)
-    return grad_tokens, widen(codes).reshape(8192, 128)
+    return sum_tokens(parts), widen(codes).reshape(8192, 128)
 
 
 def solution(mesh):

time: 157 us -> 140 us (0.89)
  blocking collectives: 49.1 us -> 21.5 us
  starting transfers between devices: 17.7 us -> 35.8 us
  between operations: 14.1 us -> 0.77 us
  waiting for transfers between devices: 24.3 us -> 31.2 us
  local copies, waits for them, and re-layouts: 3.94 us -> 6.08 us
  Pallas kernels: 41.3 us -> 39.5 us
    all_to_all x2 -> x0, blocking collectives: 32.2 us -> none  [the longest x1 22.2 us: local(): codes = sum_planes(lax.all_to_all(codes, 'z', 0, 0, tiled=True))]
    reduce_scatter x1 -> x0, waiting for transfers between devices: 13.6 us -> none  [local(): lax.psum_scatter(token_part, ('y', 'c'), scatter_dimension=0, tiled=True)]
    all_to_all x1 -> x2, waiting for transfers between devices: 0.01 us -> 13.1 us  [local(): codes = lax.all_to_all(codes, 'z', 0, 0, tiled=True)]
    all_to_all x0 -> x1, waiting for transfers between devices: none -> 10 us  [local(): stats = lax.all_to_all(stats, ('x', 'y', 'c'), 0, 0, tiled=True)]
    ppermute x0 -> x7, starting transfers between devices: none -> 8.35 us  [exchange(): out.append(lax.ppermute(block, ('y', 'c'), [(i, i ^ k) for i in range(8)]))]
    all_to_all x1 -> x2, starting transfers between devices: 4.27 us -> 11.7 us  [local(): codes = lax.all_to_all(codes, 'z', 0, 0, tiled=True)]
    all_to_all x0 -> x1, starting transfers between devices: none -> 5.61 us  [local(): stats = lax.all_to_all(stats, ('x', 'y', 'c'), 0, 0, tiled=True)]
    ppermute x6 -> x3, waiting for transfers between devices: 5.61 us -> 0.83 us  [shift(): return lax.ppermute(x, 'x', [(i, (i + k) % 4) for i in range(4)])]
  transfers between devices with their start and end apart: 9 -> 14, of which waited for: 4 -> 9; matrix products, arithmetic and copies ran while one was open for 3% -> 2% of each run, Pallas kernels for 15% -> 16%
where the time goes in v3:
time: 140 us; the launch traced here: 139 us
  Pallas kernels  39.5 us (28%)
  starting transfers between devices  35.8 us (26%)
  waiting for transfers between devices  31.2 us (22%)
  blocking collectives  21.5 us (15%)
  local copies, waits for them, and re-layouts  6.08 us (4%)
  other arithmetic  4.2 us (3%)
    all_gather x1, blocking collectives, local(): codes = lax.all_gather(codes, 'x', axis=0, tiled=True)  21.5 us
    pallas_call x1, Pallas kernels, centroid_grads(): pl.pallas_call(lambda *r: centroid_kernel(T, *r), in_specs=[pl.BlockSpec(...  15.1 us
    all_to_all x2, waiting for transfers between devices, local(): codes = lax.all_to_all(codes, 'z', 0, 0, tiled=True)  13.1 us
    all_to_all x2, starting transfers between devices, local(): codes = lax.all_to_all(codes, 'z', 0, 0, tiled=True)  11.7 us
    pallas_call x1, Pallas kernels, token_grads(): pl.pallas_call(lambda *r: token_kernel(rows, *r), in_specs=[pl.BlockSpec(...  11.5 us
    all_to_all x1, waiting for transfers between devices, local(): stats = lax.all_to_all(stats, ('x', 'y', 'c'), 0, 0, tiled=True)  10 us
    pallas_call x1, Pallas kernels, pass_one(): pl.pallas_call(lambda *r: pass_one_kernel(rows, *r), in_specs=[VM] * 3, o...  8.98 us
    ppermute x7, starting transfers between devices, exchange(): out.append(lax.ppermute(block, ('y', 'c'), [(i, i ^ k) for i in range(8)]))  8.35 us
  transfers between devices with their start and end apart: 14, of which 9 were waited for; matrix products, arithmetic and copies ran while one was open for 2% of the time, Pallas kernels for 16%

profile of v3, /device:TPU:1, one launch (start us, length us, event | category | flops | bytes accessed | tf_op | source)
XLA Modules:
  0.0 139.1 jit_solution(13059141729819920621)
XLA Ops:
  0.6 1.5 %broadcast_in_dim.4 = bf16[8,128,128]{2,1,0:T(8,128)(2,1)} broadcast(bf16[128,128]{1,0:T(8,128)(2,1)} %param.4), dimensions={1,2} | broadcast | bytes 294912 | tf_op jit(solution)/shard_map/broadcast_in_dim | solution.py:316
  2.1 6.6 %all-to-all-start = ((bf16[8,128,128]{2,1,0:T(8,128)(2,1)}), bf16[8,128,128]{2,1,0:T(8,128)(2,1)S(1)}, u32[]{:S(2)}, u32[]{:S(2)}) async-start(bf16[8,128,128]{2,1,0:T(8,128)(2,1)} %broadcast_in_dim.4), calls=%async_computation | async-start | bytes 524288 | tf_op jit(solution)/shard_map/all_to_all | solution.py:317
  10.1 5.1 %all-to-all-done = bf16[8,128,128]{2,1,0:T(8,128)(2,1)S(1)} async-done(((bf16[8,128,128]{2,1,0:T(8,128)(2,1)}), bf16[8,128,128]{2,1,0:T(8,128)(2,1)S(1)}, u32[]{:S(2)}, u32[]{:S(2)}) %all-to-all-start) | async-done | bytes 262176 | tf_op jit(solution)/shard_map/all_to_all | solution.py:317
  15.2 2.1 %collective-permute-start.2 = (bf16[1024,128]{1,0:T(8,128)(2,1)S(1)}, bf16[1024,128]{1,0:T(8,128)(2,1)S(1)}, u32[]{:S(2)}, u32[]{:S(2)}) collective-permute-start(bf16[1024,128]{1,0:T(8,128)(2,1)S(1)} %bitcast.28), channel_id=1, source_target_pairs={{0,16},{8,24},{16,0},{24,8},{1,17},{9,25},{17,1},{25,9},{2,18},{10... | collective-permute-start | bytes 786440 | tf_op jit(solution)/shard_map/ppermute | solution.py:298
  18.8 1.6 %copy-done = bf16[8192,128]{1,0:T(8,128)(2,1)S(1)} copy-done((bf16[8192,128]{1,0:T(8,128)(2,1)S(1)}, bf16[8192,128]{1,0:T(8,128)(2,1)}, u32[]{:S(2)}) %copy-start) | copy-done | bytes 2097176
  20.4 9.0 %pass_one.1 = f32[32,24,128]{2,1,0:T(8,128)} custom-call(bf16[1024,128]{1,0:T(8,128)(2,1)S(1)} %bitcast.31, bf16[8192,128]{1,0:T(8,128)(2,1)S(1)} %copy-done, f32[8,128]{1,0:T(8,128)S(1)} %maximum_maximum_fusion.r_2_), custom_call_target="tpu_custom_call" | custom-call | flops 8589934592 | bytes 2097152 | tf_op jit(solution)/shard_map/pass_one/pallas_call | solution.py:85
  30.9 5.6 %all-to-all-start.1 = ((f32[32,24,128]{2,1,0:T(8,128)}), f32[32,24,128]{2,1,0:T(8,128)S(1)}, u32[]{:S(2)}, u32[]{:S(2)}) async-start(f32[32,24,128]{2,1,0:T(8,128)} %pass_one.1), calls=%async_computation.1 | async-start | bytes 786432 | tf_op jit(solution)/shard_map/all_to_all | solution.py:321
  36.6 10.0 %all-to-all-done.1.r_5_.r_2_ = f32[32,24,128]{2,1,0:T(8,128)S(1)} async-done(((f32[32,24,128]{2,1,0:T(8,128)}), f32[32,24,128]{2,1,0:T(8,128)S(1)}, u32[]{:S(2)}, u32[]{:S(2)}) %all-to-all-start.1) | async-done | bytes 393248 | tf_op jit(solution)/shard_map/all_to_all | solution.py:321
  46.7 0.9 copy-done.3
  47.6 15.1 %centroid_grads.1 = s16[8,144,256]{2,1,0:T(8,128)(2,1)} custom-call(s32[3]{0:T(128)S(1)} %pad_add_fusion.r_0_, bf16[1024,128]{1,0:T(8,128)(2,1)S(1)} %bitcast.32, bf16[1024,128]{1,0:T(8,128)(2,1)S(1)} %copy-done.3, bf16[1024,128]{1,0:T(8,128)(2,1)S(1)} %collective-permute-done.1.r_3_, bf16[1024,128]{1,0:T(8,128)(2,1)S(1)} %collective-permute-done.2.r_4_, ...), custom_call_target="tpu_custom_call" | custom-call | flops 12884901888 | bytes 2097152 | tf_op jit(solution)/shard_map/centroid_grads/pallas_call | solution.py:231
  62.7 8.2 %all-to-all-start.2 = ((s16[8,144,256]{2,1,0:T(8,128)(2,1)}), s16[8,144,256]{2,1,0:T(8,128)(2,1)}, u32[]{:S(2)}, u32[]{:S(2)}) async-start(s16[8,144,256]{2,1,0:T(8,128)(2,1)} %centroid_grads.1), calls=%async_computation.2 | async-start | bytes 1179648 | tf_op jit(solution)/shard_map/all_to_all | solution.py:326
  70.9 11.5 %token_grads.1 = s16[8,144,128]{2,1,0:T(8,128)(2,1)S(1)} custom-call(s32[3]{0:T(128)S(1)} %pad_add_fusion.r_0_, bf16[1024,128]{1,0:T(8,128)(2,1)S(1)} %bitcast.33, f32[32,24,128]{2,1,0:T(8,128)S(1)} %all-to-all-done.1.r_5_.r_2_, bf16[8192,128]{1,0:T(8,128)(2,1)S(1)} %copy-done.1), custom_call_target="tpu_custom_call" | custom-call | flops 12884901888 | bytes 2097152 | tf_op jit(solution)/shard_map/token_grads/pallas_call | solution.py:161
  82.5 8.0 %all-to-all-done.2.in_ref = s16[8,144,256]{2,1,0:T(8,128)(2,1)} async-done(((s16[8,144,256]{2,1,0:T(8,128)(2,1)}), s16[8,144,256]{2,1,0:T(8,128)(2,1)}, u32[]{:S(2)}, u32[]{:S(2)}) %all-to-all-start.2) | async-done | bytes 589856 | tf_op jit(solution)/shard_map/all_to_all | solution.py:326
  90.5 2.2 %sum_planes.1 = s16[8,272,128]{2,1,0:T(8,128)(2,1)} custom-call(s16[8,144,256]{2,1,0:T(8,128)(2,1)} %all-to-all-done.2.in_ref), custom_call_target="tpu_custom_call" | custom-call | flops 4194304 | bytes 2097152 | tf_op jit(solution)/shard_map/sum_planes/pallas_call | solution.py:283
  92.7 3.5 %all-to-all-start.3 = ((s16[8,272,128]{2,1,0:T(8,128)(2,1)}), s16[8,272,128]{2,1,0:T(8,128)(2,1)S(1)}, u32[]{:S(2)}, u32[]{:S(2)}) async-start(s16[8,272,128]{2,1,0:T(8,128)(2,1)} %sum_planes.1), calls=%async_computation.3 | async-start | bytes 1114112 | tf_op jit(solution)/shard_map/all_to_all | solution.py:331
  96.9 1.4 collective-permute-start.9
  98.3 1.7 %collective-permute-start.8 = (s16[144,128]{1,0:T(8,128)(2,1)S(1)}, s16[144,128]{1,0:T(8,128)(2,1)S(1)}, u32[]{:S(2)}, u32[]{:S(2)}) collective-permute-start(s16[144,128]{1,0:T(8,128)(2,1)S(1)} %get-tuple-element.17), channel_id=1, source_target_pairs={{0,6},{1,7},{2,4},{3,5},{4,2},{5,3},{6,0},{7,1},{8,14},{9,15},{10,... | collective-permute-start | bytes 110600 | tf_op jit(solution)/shard_map/ppermute | solution.py:309
  99.9 3.2 %collective-permute-start.6 = (s16[144,128]{1,0:T(8,128)(2,1)S(1)}, s16[144,128]{1,0:T(8,128)(2,1)S(1)}, u32[]{:S(2)}, u32[]{:S(2)}) collective-permute-start(s16[144,128]{1,0:T(8,128)(2,1)S(1)} %get-tuple-element.19), channel_id=1, source_target_pairs={{0,4},{1,5},{2,6},{3,7},{4,0},{5,1},{6,2},{7,3},{8,12},{9,13},{10,... | collective-permute-start | bytes 110600 | tf_op jit(solution)/shard_map/ppermute | solution.py:309
  103.1 1.8 %collective-permute-start.4 = (s16[144,128]{1,0:T(8,128)(2,1)S(1)}, s16[144,128]{1,0:T(8,128)(2,1)S(1)}, u32[]{:S(2)}, u32[]{:S(2)}) collective-permute-start(s16[144,128]{1,0:T(8,128)(2,1)S(1)} %get-tuple-element.21), channel_id=1, source_target_pairs={{0,2},{1,3},{2,0},{3,1},{4,6},{5,7},{6,4},{7,5},{8,10},{9,11},{10,... | collective-permute-start | bytes 110600 | tf_op jit(solution)/shard_map/ppermute | solution.py:309
  105.7 1.5 %collective-permute-done.5.refs_3_ = s16[144,128]{1,0:T(8,128)(2,1)S(1)} collective-permute-done((s16[144,128]{1,0:T(8,128)(2,1)S(1)}, s16[144,128]{1,0:T(8,128)(2,1)S(1)}, u32[]{:S(2)}, u32[]{:S(2)}) %collective-permute-start.5) | collective-permute-done | bytes 36896 | tf_op jit(solution)/shard_map/ppermute | solution.py:309
  108.1 1.7 %sum_tokens.1 = f32[128,128]{1,0:T(8,128)} custom-call(s16[144,128]{1,0:T(8,128)(2,1)} %get-tuple-element.23.refs_0_, s16[144,128]{1,0:T(8,128)(2,1)} %copy-done.10, s16[144,128]{1,0:T(8,128)(2,1)} %copy-done.9, s16[144,128]{1,0:T(8,128)(2,1)} %copy-done.8, s16[144,128]{1,0:T(8,128)(2,1)} %copy-done.7, s16[144,128]{1,0:T(8,128)(2,1)} %copy-done.6, ...), custom_call_target="tpu_custom_call" | custom-call | flops 262144 | bytes 2097152 | tf_op jit(solution)/shard_map/sum_tokens/pallas_call | solution.py:265
  109.8 5.1 %all-to-all-done.3 = s16[8,272,128]{2,1,0:T(8,128)(2,1)S(1)} async-done(((s16[8,272,128]{2,1,0:T(8,128)(2,1)}), s16[8,272,128]{2,1,0:T(8,128)(2,1)S(1)}, u32[]{:S(2)}, u32[]{:S(2)}) %all-to-all-start.3) | async-done | bytes 557088 | tf_op jit(solution)/shard_map/all_to_all | solution.py:331
  114.8 21.5 %all-gather.1 = s16[32,272,128]{2,1,0:T(8,128)(2,1)S(1)} all-gather(s16[8,272,128]{2,1,0:T(8,128)(2,1)S(1)} %all-to-all-done.3), channel_id=1, replica_groups=mesh['z'=8,'x'=4,'y'=4,'c'=2] {'x'}, dimensions={0}, use_global_device_ids=true | all-gather | bytes 2785280 | tf_op jit(solution)/shard_map/all_gather | solution.py:332
  136.4 2.7 %convert_multiply_fusion = f32[32,256,128]{2,1,0:T(8,128)} fusion(s16[32,272,128]{2,1,0:T(8,128)(2,1)S(1)} %all-gather.1, f32[32,128]{1,0:T(8,128)S(1)} %multiply_bitcast_fusion), kind=kLoop, calls=%fused_computation | loop fusion | flops 2097152 | bytes 6307840 | tf_op jit(solution)/shard_map/mul | solution.py:294
  (43 shorter events, 6.9 us)
Async XLA Ops:
  2.1 13.1 %all-to-all-start = ((bf16[8,128,128]{2,1,0:T(8,128)(2,1)}), bf16[8,128,128]{2,1,0:T(8,128)(2,1)S(1)}, u32[]{:S(2)}, u32[]{:S(2)}) async-start(bf16[8,128,128]{2,1,0:T(8,128)(2,1)} %broadcast_in_dim.4), calls=%async_computation | async-start | bytes 524288 | tf_op jit(solution)/shard_map/all_to_all | solution.py:317
  15.2 14.2 %collective-permute-start.2 = (bf16[1024,128]{1,0:T(8,128)(2,1)S(1)}, bf16[1024,128]{1,0:T(8,128)(2,1)S(1)}, u32[]{:S(2)}, u32[]{:S(2)}) collective-permute-start(bf16[1024,128]{1,0:T(8,128)(2,1)S(1)} %bitcast.28), channel_id=1, source_target_pairs={{0,16},{8,24},{16,0},{24,8},{1,17},{9,25},{17,1},{25,9},{2,18},{10... | collective-permute-start | bytes 786440 | tf_op jit(solution)/shard_map/ppermute | solution.py:298
  17.3 12.1 %collective-permute-start.1 = (bf16[1024,128]{1,0:T(8,128)(2,1)S(1)}, bf16[1024,128]{1,0:T(8,128)(2,1)S(1)}, u32[]{:S(2)}, u32[]{:S(2)}) collective-permute-start(bf16[1024,128]{1,0:T(8,128)(2,1)S(1)} %bitcast.29), channel_id=1, source_target_pairs={{0,24},{8,0},{16,8},{24,16},{1,25},{9,1},{17,9},{25,17},{2,26},{10... | collective-permute-start | bytes 786440 | tf_op jit(solution)/shard_map/ppermute | solution.py:298
  18.2 12.0 %collective-permute-start = (bf16[1024,128]{1,0:T(8,128)(2,1)S(1)}, bf16[1024,128]{1,0:T(8,128)(2,1)S(1)}, u32[]{:S(2)}, u32[]{:S(2)}) collective-permute-start(bf16[1024,128]{1,0:T(8,128)(2,1)S(1)} %bitcast.30), channel_id=1, source_target_pairs={{0,8},{8,16},{16,24},{24,0},{1,9},{9,17},{17,25},{25,1},{2,10},{10... | collective-permute-start | bytes 786440 | tf_op jit(solution)/shard_map/ppermute | solution.py:298
  18.8 1.6 %copy-start = (bf16[8192,128]{1,0:T(8,128)(2,1)S(1)}, bf16[8192,128]{1,0:T(8,128)(2,1)}, u32[]{:S(2)}) copy-start(bf16[8192,128]{1,0:T(8,128)(2,1)} %r_3_.1) | copy-start | bytes 6291460
  20.4 26.3 %copy-start.1 = (bf16[8192,128]{1,0:T(8,128)(2,1)S(1)}, bf16[8192,128]{1,0:T(8,128)(2,1)}, u32[]{:S(2)}) copy-start(bf16[8192,128]{1,0:T(8,128)(2,1)} %r_3_.1) | copy-start | bytes 6291460
  30.2 0.7 copy-start.2
  30.9 15.7 %all-to-all-start.1 = ((f32[32,24,128]{2,1,0:T(8,128)}), f32[32,24,128]{2,1,0:T(8,128)S(1)}, u32[]{:S(2)}, u32[]{:S(2)}) async-start(f32[32,24,128]{2,1,0:T(8,128)} %pass_one.1), calls=%async_computation.1 | async-start | bytes 786432 | tf_op jit(solution)/shard_map/all_to_all | solution.py:321
  46.7 1.0 copy-start.3
  62.7 27.7 %all-to-all-start.2 = ((s16[8,144,256]{2,1,0:T(8,128)(2,1)}), s16[8,144,256]{2,1,0:T(8,128)(2,1)}, u32[]{:S(2)}, u32[]{:S(2)}) async-start(s16[8,144,256]{2,1,0:T(8,128)(2,1)} %centroid_grads.1), calls=%async_computation.2 | async-start | bytes 1179648 | tf_op jit(solution)/shard_map/all_to_all | solution.py:326
  92.7 22.2 %all-to-all-start.3 = ((s16[8,272,128]{2,1,0:T(8,128)(2,1)}), s16[8,272,128]{2,1,0:T(8,128)(2,1)S(1)}, u32[]{:S(2)}, u32[]{:S(2)}) async-start(s16[8,272,128]{2,1,0:T(8,128)(2,1)} %sum_planes.1), calls=%async_computation.3 | async-start | bytes 1114112 | tf_op jit(solution)/shard_map/all_to_all | solution.py:331
  96.9 6.2 %collective-permute-start.9 = (s16[144,128]{1,0:T(8,128)(2,1)S(1)}, s16[144,128]{1,0:T(8,128)(2,1)S(1)}, u32[]{:S(2)}, u32[]{:S(2)}) collective-permute-start(s16[144,128]{1,0:T(8,128)(2,1)S(1)} %get-tuple-element.16), channel_id=1, source_target_pairs={{0,7},{1,6},{2,5},{3,4},{4,3},{5,2},{6,1},{7,0},{8,15},{9,14},{10,... | collective-permute-start | bytes 110600 | tf_op jit(solution)/shard_map/ppermute | solution.py:309
  98.3 6.7 %collective-permute-start.8 = (s16[144,128]{1,0:T(8,128)(2,1)S(1)}, s16[144,128]{1,0:T(8,128)(2,1)S(1)}, u32[]{:S(2)}, u32[]{:S(2)}) collective-permute-start(s16[144,128]{1,0:T(8,128)(2,1)S(1)} %get-tuple-element.17), channel_id=1, source_target_pairs={{0,6},{1,7},{2,4},{3,5},{4,2},{5,3},{6,0},{7,1},{8,14},{9,15},{10,... | collective-permute-start | bytes 110600 | tf_op jit(solution)/shard_map/ppermute | solution.py:309
  99.9 5.5 %collective-permute-start.7 = (s16[144,128]{1,0:T(8,128)(2,1)S(1)}, s16[144,128]{1,0:T(8,128)(2,1)S(1)}, u32[]{:S(2)}, u32[]{:S(2)}) collective-permute-start(s16[144,128]{1,0:T(8,128)(2,1)S(1)} %get-tuple-element.18), channel_id=1, source_target_pairs={{0,5},{1,4},{2,7},{3,6},{4,1},{5,0},{6,3},{7,2},{8,13},{9,12},{10,... | collective-permute-start | bytes 110600 | tf_op jit(solution)/shard_map/ppermute | solution.py:309
  99.9 5.7 %collective-permute-start.6 = (s16[144,128]{1,0:T(8,128)(2,1)S(1)}, s16[144,128]{1,0:T(8,128)(2,1)S(1)}, u32[]{:S(2)}, u32[]{:S(2)}) collective-permute-start(s16[144,128]{1,0:T(8,128)(2,1)S(1)} %get-tuple-element.19), channel_id=1, source_target_pairs={{0,4},{1,5},{2,6},{3,7},{4,0},{5,1},{6,2},{7,3},{8,12},{9,13},{10,... | collective-permute-start | bytes 110600 | tf_op jit(solution)/shard_map/ppermute | solution.py:309
  103.1 4.1 %collective-permute-start.5 = (s16[144,128]{1,0:T(8,128)(2,1)S(1)}, s16[144,128]{1,0:T(8,128)(2,1)S(1)}, u32[]{:S(2)}, u32[]{:S(2)}) collective-permute-start(s16[144,128]{1,0:T(8,128)(2,1)S(1)} %get-tuple-element.20), channel_id=1, source_target_pairs={{0,3},{1,2},{2,1},{3,0},{4,7},{5,6},{6,5},{7,4},{8,11},{9,10},{10,... | collective-permute-start | bytes 110600 | tf_op jit(solution)/shard_map/ppermute | solution.py:309
  103.1 4.4 %copy-start.4 = (s16[144,128]{1,0:T(8,128)(2,1)}, s16[144,128]{1,0:T(8,128)(2,1)S(1)}, u32[]{:S(2)}) copy-start(s16[144,128]{1,0:T(8,128)(2,1)S(1)} %collective-permute-done.9.refs_7_) | copy-start | bytes 110596
  103.1 4.4 %collective-permute-start.4 = (s16[144,128]{1,0:T(8,128)(2,1)S(1)}, s16[144,128]{1,0:T(8,128)(2,1)S(1)}, u32[]{:S(2)}, u32[]{:S(2)}) collective-permute-start(s16[144,128]{1,0:T(8,128)(2,1)S(1)} %get-tuple-element.21), channel_id=1, source_target_pairs={{0,2},{1,3},{2,0},{3,1},{4,6},{5,7},{6,4},{7,5},{8,10},{9,11},{10,... | collective-permute-start | bytes 110600 | tf_op jit(solution)/shard_map/ppermute | solution.py:309
  104.9 2.6 %copy-start.5 = (s16[144,128]{1,0:T(8,128)(2,1)}, s16[144,128]{1,0:T(8,128)(2,1)S(1)}, u32[]{:S(2)}) copy-start(s16[144,128]{1,0:T(8,128)(2,1)S(1)} %collective-permute-done.8.refs_6_) | copy-start | bytes 110596
  104.9 2.6 %collective-permute-start.3 = (s16[144,128]{1,0:T(8,128)(2,1)S(1)}, s16[144,128]{1,0:T(8,128)(2,1)S(1)}, u32[]{:S(2)}, u32[]{:S(2)}) collective-permute-start(s16[144,128]{1,0:T(8,128)(2,1)S(1)} %get-tuple-element.22), channel_id=1, source_target_pairs={{0,1},{1,0},{2,3},{3,2},{4,5},{5,4},{6,7},{7,6},{8,9},{9,8},{10,11... | collective-permute-start | bytes 110600 | tf_op jit(solution)/shard_map/ppermute | solution.py:309
  105.4 2.1 %copy-start.6 = (s16[144,128]{1,0:T(8,128)(2,1)}, s16[144,128]{1,0:T(8,128)(2,1)S(1)}, u32[]{:S(2)}) copy-start(s16[144,128]{1,0:T(8,128)(2,1)S(1)} %collective-permute-done.7.refs_5_) | copy-start | bytes 110596
  105.7 1.9 %copy-start.7 = (s16[144,128]{1,0:T(8,128)(2,1)}, s16[144,128]{1,0:T(8,128)(2,1)S(1)}, u32[]{:S(2)}) copy-start(s16[144,128]{1,0:T(8,128)(2,1)S(1)} %collective-permute-done.6.refs_4_) | copy-start | bytes 110596
  107.2 0.6 copy-start.8
  107.5 0.6 copy-start.10
  (1 other events, 0.6 us)
